TPU v7x, 32 devices: a whole 2x2x4 slice. The times are simulated.
32 devices in a mesh: group: 2 (over x), dp: 16 (over z, y, core).
Axes of the slice: x: 2, y: 2, z: 4, core: 2. Of those that a mesh axis runs over, the one named last changes fastest.
Arguments:
- candidate_queries: bfloat16 [256, 8, 16, 4096], P(('group', 'dp')), parts along dimension 0, may hold values from -10 to 10
- target_states: bfloat16 [256, 32, 1024], P(('group', 'dp')), parts along dimension 0, may hold values from -4 to 4
- target_queries: bfloat16 [256, 32, 4096], P(('group', 'dp')), parts along dimension 0, may hold values from -10 to 10
- candidate_states: bfloat16 [2048, 16, 1024], P(('group', 'dp')), parts along dimension 0, may hold values from -4 to 4
- target_length: int32 [256], P(('group', 'dp')), parts along dimension 0, may hold values from 2 to 32
- candidate_length: int32 [256, 8], P(('group', 'dp')), parts along dimension 0, may hold values from 2 to 16
- candidate_row: int32 [256, 8], P(('group', 'dp')), parts along dimension 0, may hold values from 0 to 63, as said below
- direct_readout: bfloat16 [4096], replicated, may hold values from -0.5 to 0.5
- channel_readout: bfloat16 [4096], replicated, may hold values from -0.5 to 0.5
Outputs:
- rescored: float32 [2048], P(('group', 'dp')), parts along dimension 0
There are 2 independent parts, one for each index of `group`. A program takes and returns all parts, laid end to end along the dimension named above; an argument that names none is the same for every part. Nothing has to cross between parts.
Inputs may be any that keep to these rules, and one draw needn't show every extreme that they name: `candidate_row`: on the 8 targets of each aligned block (targets b * 8 to (b + 1) * 8 - 1), the 64 entries hold every value from 0 to 63 once.
All inputs are finite; a program needn't handle non-finite values.
Results may differ from a plain program's by a relative error of at most 0.0021.
Values may be sent and summed in bfloat16 or wider, within the bound.
No kernel may reach another device: no remote copies, remote signals or barrier semaphores. Data moves between devices by JAX's collectives and lax.ppermute only.
A program may use at most 128 MiB of HBM per device.

v0:
```python
import math

import jax
import jax.numpy as jnp
from jax import lax
from jax.sharding import PartitionSpec as P

QUERY_HEADS = 32
KEY_VALUE_HEADS = 4
HEAD_SIZE = 128


masked_score = -1e30


def softmax_weights(scores, usable):
    scores = jnp.where(usable, scores, masked_score)
    highest = jnp.max(scores, axis=-1, keepdims=True)
    weights = jnp.exp(scores - highest)
    return (weights / jnp.sum(weights, axis=-1, keepdims=True)).astype(jnp.bfloat16)


def attend_shared(query_rows, hidden_states, length):
    batch_groups, count_of_rows, model_width = query_rows.shape
    length_of_keys = hidden_states.shape[1]
    grouped_heads = query_rows.reshape(
        batch_groups, count_of_rows, KEY_VALUE_HEADS, QUERY_HEADS // KEY_VALUE_HEADS, HEAD_SIZE
    )
    split_halves = hidden_states.reshape(
        batch_groups, length_of_keys, 2, KEY_VALUE_HEADS, HEAD_SIZE
    )
    scores = jnp.einsum(
        "brgqd,bkgd->bgqrk",
        grouped_heads,
        split_halves[:, :, 0],
        preferred_element_type=jnp.float32,
    ) * (1.0 / math.sqrt(HEAD_SIZE))
    usable = (jnp.arange(length_of_keys, dtype=jnp.int32)[None, :] < length[:, None])[
        :, None, None, None, :
    ]
    weights = softmax_weights(scores, usable)
    mixture = jnp.einsum(
        "bgqrk,bkgd->brgqd", weights, split_halves[:, :, 1], preferred_element_type=jnp.float32
    )
    return mixture.astype(jnp.bfloat16).reshape(batch_groups, count_of_rows, model_width)


def attend_paired(query_rows, hidden_states, length):
    batch_groups, count_of_rows, model_width = query_rows.shape
    count_of_pairs, length_of_keys = (hidden_states.shape[1], hidden_states.shape[2])
    grouped_heads = query_rows.reshape(
        batch_groups, count_of_rows, KEY_VALUE_HEADS, QUERY_HEADS // KEY_VALUE_HEADS, HEAD_SIZE
    )
    split_halves = hidden_states.reshape(
        batch_groups, count_of_pairs, length_of_keys, 2, KEY_VALUE_HEADS, HEAD_SIZE
    )
    scores = jnp.einsum(
        "brgqd,bpkgd->bpgqrk",
        grouped_heads,
        split_halves[:, :, :, 0],
        preferred_element_type=jnp.float32,
    ) * (1.0 / math.sqrt(HEAD_SIZE))
    usable = (jnp.arange(length_of_keys, dtype=jnp.int32)[None, None, :] < length[:, :, None])[
        :, :, None, None, None, :
    ]
    weights = softmax_weights(scores, usable)
    mixture = jnp.einsum(
        "bpgqrk,bpkgd->bprgqd",
        weights,
        split_halves[:, :, :, 1],
        preferred_element_type=jnp.float32,
    )
    return mixture.astype(jnp.bfloat16).reshape(
        batch_groups, count_of_pairs, count_of_rows, model_width
    )


def pooled(mixture, readout, length):
    tokens = jnp.dot(mixture, readout, preferred_element_type=jnp.float32)
    usable = jnp.arange(tokens.shape[-1], dtype=jnp.int32) < length[..., None]
    return jnp.sum(jnp.where(usable, tokens, 0.0), axis=-1) / length.astype(jnp.float32)


def on_device(
    candidate_queries,
    target_states,
    target_queries,
    candidate_states,
    target_length,
    candidate_length,
    candidate_row,
    direct_readout,
    channel_readout,
):
    target_count, slot_count, source_length, model_width = candidate_queries.shape
    candidate_count = target_count * slot_count
    direct_mix = attend_shared(
        candidate_queries.reshape(target_count, slot_count * source_length, model_width),
        target_states,
        target_length,
    )
    direct = pooled(
        direct_mix.reshape(target_count, slot_count, source_length, model_width),
        direct_readout,
        candidate_length,
    )
    flat_rows = candidate_row.reshape(candidate_count)
    matches = flat_rows[None, :] == jnp.arange(candidate_count, dtype=jnp.int32)[:, None]
    arrived = lax.all_to_all(candidate_states, "dp", split_axis=0, concat_axis=0, tiled=True)
    paired = jnp.take(arrived, flat_rows, axis=0).reshape(
        target_count, slot_count, source_length, arrived.shape[2]
    )
    channel_mix = attend_paired(target_queries, paired, candidate_length)
    target_counts = jnp.broadcast_to(target_length[:, None], candidate_length.shape)
    channel = pooled(channel_mix, channel_readout, target_counts)
    combined = (direct + channel).reshape(candidate_count)
    outgoing = jnp.sum(jnp.where(matches, combined[None, :], 0.0), axis=1)
    result = lax.all_to_all(outgoing, "dp", split_axis=0, concat_axis=0, tiled=True)
    return result


def solution(mesh):
    in_specs = (
        P(("group", "dp"), None, None, None),
        P(("group", "dp"), None, None),
        P(("group", "dp"), None, None),
        P(("group", "dp"), None, None),
        P(("group", "dp")),
        P(("group", "dp"), None),
        P(("group", "dp"), None),
        P(),
        P(),
    )
    out_specs = P(("group", "dp"))
    return jax.shard_map(
        on_device, mesh=mesh, in_specs=in_specs, out_specs=out_specs, check_vma=False
    )
```

profile of v0, /device:TPU:0, one launch (start us, length us, event | category | flops | bytes accessed | tf_op | source)
XLA Modules:
  0.0 181.2 jit_solution(12942013003783667898)
XLA Ops:
  0.0 7.5 %all-to-all-start = ((bf16[64,16,1024]{2,1,0:T(8,128)(2,1)}), bf16[64,16,1024]{2,1,0:T(8,128)(2,1)S(1)}, u32[]{:S(2)}, u32[]{:S(2)}) async-start(bf16[64,16,1024]{2,1,0:T(8,128)(2,1)} %param.12), calls=%async_computation | async-start | bytes 4194304 | tf_op jit(solution)/shard_map/all_to_all | solution.py:109
  7.7 3.4 %copy.59 = bf16[32,8,32,128]{3,2,1,0:T(8,128)(2,1)} copy(bf16[32,8,32,128]{3,1,2,0:T(8,128)(2,1)} %bitcast.90) | data formatting | bytes 4194304
  11.2 0.4 reshape.77
  11.6 9.4 %copy.58 = bf16[128,8,32,128]{3,2,1,0:T(8,128)(2,1)} copy(bf16[128,8,32,128]{3,1,2,0:T(8,128)(2,1)} %bitcast.89) | data formatting | bytes 16777216
  21.1 0.2 fusion.39
  21.3 6.4 %fusion.7 = f32[8,4,32,128,8]{3,2,4,1,0:T(8,128)S(1)} fusion(bf16[8,128,4,8,128]{4,3,2,1,0:T(8,128)(2,1)} %bitcast.88, bf16[8,32,1,4,128]{4,3,2,1,0:T(4,128)(2,1)S(1)} %get-tuple-element.6), kind=kOutput, calls=%fused_computation.11 | convolution fusion | flops 268435456 | bytes 12845056 | tf_op jit(solution)/shard_map/brgqd,bkgd->bgqrk/dot_general | solution.py:32
  27.7 2.2 %fusion.45 = (f32[8,4,8,128]{3,2,1,0:T(8,128)S(1)}, f32[8,4,8,128,32]{3,4,2,1,0:T(8,128)S(1)}) fusion(f32[8,4,32,128,8]{3,2,4,1,0:T(8,128)S(1)} %fusion.7, pred[8,32]{1,0:T(8,128)(4,1)S(1)} %iota_compare_fusion.3), kind=kOutput, calls=%fused_computation.60 | output fusion | flops 6291487 | bytes 8519936 | tf_op jit(solution)/shard_map/sub | solution.py:19
  29.9 4.7 %convert_bitcast_fusion.1 = bf16[8,128,4,8,128]{4,1,3,2,0:T(8,128)(2,1)} fusion(f32[8,4,8,128,32]{3,4,2,1,0:T(8,128)S(1)} %get-tuple-element.10, f32[8,4,8,128]{3,2,1,0:T(8,128)S(1)} %get-tuple-element.9, bf16[8,32,1,4,128]{4,3,2,1,0:T(4,128)(2,1)S(1)} %get-tuple-element.5), kind=kOutput, calls=%fused_computation.15 | convolution fusion | flops 274726912 | bytes 12976128 | tf_op jit(solution)/shard_map/bgqrk,bkgd->brgqd/dot_general | solution.py:42
  34.7 12.0 %copy.36 = bf16[8,128,4,8,128]{4,3,2,1,0:T(8,128)(2,1)} copy(bf16[8,128,4,8,128]{4,1,3,2,0:T(8,128)(2,1)} %convert_bitcast_fusion.1) | data formatting | bytes 16777216 | tf_op jit(solution)/shard_map/convert_element_type | solution.py:45
  46.7 13.3 %reshape_reshape.8 = bf16[8,8,16,4096]{3,2,1,0:T(8,128)(2,1)} reshape(bf16[8,128,4,8,128]{4,3,2,1,0:T(8,128)(2,1)} %copy.36) | data formatting | bytes 16777216 | tf_op jit(solution)/shard_map/reshape;reshape | solution.py:103
  60.1 13.2 %fusion.32 = f32[1,8,8,16]{3,0,2,1:T(1,128)S(1)} fusion(bf16[8,8,16,4096]{3,2,1,0:T(8,128)(2,1)} %reshape_reshape.8, bf16[4096,1,1,1]{0,1,2,3:T(2,128)(2,1)S(1)} %reshape.91), kind=kOutput, calls=%fused_computation.45 | convolution fusion | flops 8388608 | bytes 8400896 | tf_op jit(solution)/shard_map/dot_general | solution.py:79
  73.3 0.2 select_reduce_fusion.2
  73.5 2.0 %gather_fusion = bf16[64,16,1024]{2,1,0:T(8,128)(2,1)} fusion(bf16[64,16,1024]{2,1,0:T(8,128)(2,1)S(1)} %all-to-all-done, s32[1024]{0:T(1024)S(1)} %pad_clamp_fusion), kind=kCustom, calls=%fused_computation | custom fusion | bytes 4194560 | tf_op jit(solution)/shard_map/jit(_take)/gather | solution.py:110
  75.6 3.2 %gather.7 = bf16[8,8,16,2,4,128]{5,4,3,2,1,0:T(4,128)(2,1)S(1)} reshape(bf16[64,16,1024]{2,1,0:T(8,128)(2,1)} %gather_fusion) | data formatting | bytes 4194304 | tf_op jit(solution)/shard_map/jit(_take)/gather | solution.py:110
  78.8 1.6 copy_select_fusion
  80.4 15.7 %fusion.40 = (f32[8,8,4,8,32]{4,3,1,2,0:T(8,128)}, f32[8,8,4,8,32,16]{4,5,3,1,2,0:T(8,128)}) fusion(pred[8,8,16]{2,1,0:T(8,128)(4,1)S(1)} %iota_compare_fusion.1, bf16[8,32,4,8,128,1]{4,3,2,1,0,5:T(8,128)(2,1)} %bitcast.91, bf16[8,8,16,2,4,128]{5,2,1,4,0,3:T(8,128)(2,1)} %copy_select_fusion), kind=kOutput, calls=%fused_computation.59 | convolution fusion | flops 272629760 | bytes 7603200 | tf_op jit(solution)/shard_map/sub | solution.py:19
  96.1 13.3 %convert_bitcast_fusion = bf16[8,8,32,4,8,128]{5,2,4,3,1,0:T(8,128)(2,1)} fusion(f32[8,8,4,8,32,16]{4,5,3,1,2,0:T(8,128)} %get-tuple-element.8, f32[8,8,4,8,32]{4,3,1,2,0:T(8,128)} %get-tuple-element.7, bf16[8,8,16,2,4,128]{5,2,1,4,0,3:T(8,128)(2,1)S(1)} %copy-done), kind=kOutput, calls=%fused_computation.7 | convolution fusion | flops 278921216 | bytes 22282240 | tf_op jit(solution)/shard_map/bpgqrk,bpkgd->bprgqd/dot_general | solution.py:67
  109.5 17.5 %copy.41 = bf16[8,8,32,4,8,128]{5,4,3,2,1,0:T(8,128)(2,1)} copy(bf16[8,8,32,4,8,128]{5,2,4,3,1,0:T(8,128)(2,1)} %convert_bitcast_fusion) | data formatting | bytes 33554432 | tf_op jit(solution)/shard_map/convert_element_type | solution.py:73
  127.0 25.3 %reshape.80 = bf16[8,8,32,4096]{3,2,1,0:T(8,128)(2,1)} reshape(bf16[8,8,32,4,8,128]{5,4,3,2,1,0:T(8,128)(2,1)} %copy.41) | data formatting | bytes 33554432 | tf_op jit(solution)/shard_map/reshape | solution.py:73
  152.3 14.4 %fusion.30 = f32[1,8,8,32]{3,0,2,1:T(1,128)S(1)} fusion(bf16[8,8,32,4096]{3,2,1,0:T(8,128)(2,1)} %reshape.80, bf16[4096,1,1,1]{0,1,2,3:T(2,128)(2,1)S(1)} %reshape.96), kind=kOutput, calls=%fused_computation.43 | convolution fusion | flops 16777216 | bytes 16793600 | tf_op jit(solution)/shard_map/dot_general | solution.py:79
  167.2 12.2 %all_to_all.17 = f32[16,4,1]{1,2,0:T(1,128)S(1)} all-to-all(f32[16,4,1]{1,2,0:T(1,128)S(1)} %bitcast.94), channel_id=1, replica_groups=mesh['group'=2,'dp'=16] {'dp'}, dimensions={0} | all-to-all | bytes 512 | tf_op jit(solution)/shard_map/all_to_all | solution.py:118
  179.5 0.5 broadcast.70
  180.0 0.7 reduce.3
  180.6 0.6 all_to_all.14
  (30 shorter events, 0.9 us)
Async XLA Ops:
  0.0 7.5 %copy-start.2 = (s32[8,8]{1,0:T(8,128)S(1)}, s32[8,8]{1,0:T(8,128)}, u32[]{:S(2)}) copy-start(s32[8,8]{1,0:T(8,128)} %param.15) | copy-start | bytes 772
  0.0 11.1 %copy-start.4 = (bf16[4096]{0:T(1024)(128)(2,1)S(1)}, bf16[4096]{0:T(1024)(128)(2,1)}, u32[]{:S(2)}) copy-start(bf16[4096]{0:T(1024)(128)(2,1)} %param.17) | copy-start | bytes 24580
  0.0 11.2 %copy-start.1 = (bf16[8,32,1024]{2,1,0:T(8,128)(2,1)S(1)}, bf16[8,32,1024]{2,1,0:T(8,128)(2,1)}, u32[]{:S(2)}) copy-start(bf16[8,32,1024]{2,1,0:T(8,128)(2,1)} %param.10) | copy-start | bytes 1572868
  0.0 73.5 %all-to-all-start = ((bf16[64,16,1024]{2,1,0:T(8,128)(2,1)}), bf16[64,16,1024]{2,1,0:T(8,128)(2,1)S(1)}, u32[]{:S(2)}, u32[]{:S(2)}) async-start(bf16[64,16,1024]{2,1,0:T(8,128)(2,1)} %param.12), calls=%async_computation | async-start | bytes 4194304 | tf_op jit(solution)/shard_map/all_to_all | solution.py:109
  11.5 9.5 %copy-start.6 = (s32[8]{0:T(128)S(1)}, s32[8]{0:T(128)}, u32[]{:S(2)}) copy-start(s32[8]{0:T(128)} %param.13) | copy-start | bytes 100
  46.7 13.3 %copy-start.5 = (bf16[4096]{0:T(1024)(128)(2,1)S(1)}, bf16[4096]{0:T(1024)(128)(2,1)}, u32[]{:S(2)}) copy-start(bf16[4096]{0:T(1024)(128)(2,1)} %param.16) | copy-start | bytes 24580
  60.1 13.2 %copy-start.3 = (s32[8,8]{1,0:T(8,128)S(1)}, s32[8,8]{1,0:T(8,128)}, u32[]{:S(2)}) copy-start(s32[8,8]{1,0:T(8,128)} %param.14) | copy-start | bytes 772
  80.4 15.7 %copy-start = (bf16[8,8,16,2,4,128]{5,2,1,4,0,3:T(8,128)(2,1)S(1)}, bf16[8,8,16,2,4,128]{5,2,1,4,0,3:T(8,128)(2,1)}, u32[]{:S(2)}) copy-start(bf16[8,8,16,2,4,128]{5,2,1,4,0,3:T(8,128)(2,1)} %copy_select_fusion) | copy-start | bytes 6291460
where the time goes:
time: 183 us; the launch traced here: 181 us
  local copies, waits for them, and re-layouts  88.3 us (48%)
  matrix products  67.8 us (37%)
  blocking collectives  12.2 us (7%)
  starting transfers between devices  7.53 us (4%)
  other arithmetic  5.21 us (3%)
    dot_general x2, matrix products, pooled(): tokens = jnp.dot(mixture, readout, preferred_element_type=jnp.float32)  27.6 us
    reshape x1, local copies, waits for them, and re-layouts, attend_paired(): mixture.astype(jnp.bfloat16)  25.3 us
    convert_element_type x1, local copies, waits for them, and re-layouts, attend_paired(): mixture.astype(jnp.bfloat16)  17.5 us
    sub x1, matrix products, softmax_weights(): weights = jnp.exp(scores - highest)  15.7 us
    dot_general x1, matrix products, attend_paired(): jnp.einsum('bpgqrk,bpkgd->bprgqd', weights, split_halves[:, :, :, 1], pre...  13.3 us
    another operation x1, local copies, waits for them, and re-layouts, on_device(): direct_mix.reshape(target_count, slot_count, source_length, model_width)  13.3 us
    unnamed x18, local copies, waits for them, and re-layouts  12.9 us
    all_to_all x1, blocking collectives, on_device(): lax.all_to_all(outgoing, 'dp', split_axis=0, concat_axis=0, tiled=True)  12.2 us
  transfers between devices with their start and end apart: 1, of which 0 were waited for; matrix products, arithmetic and copies ran while one was open for 36% of the time, Pallas kernels for 0%

commit v1 on v0

v1 whole, which is shorter than its diff:
```python
import functools
import math

import jax
import jax.numpy as jnp
from jax import lax
from jax.experimental import pallas as pl
from jax.experimental.pallas import tpu as pltpu
from jax.sharding import PartitionSpec as P

KEY_VALUE_HEADS = 4
HEAD_SIZE = 128
LANES = 128
SUBLANES = 8
MASKED = -1e30

bf16 = jnp.bfloat16
f32 = jnp.float32


def dot_nt(a, b):
    return lax.dot_general(a, b, (((1,), (1,)), ((), ())), preferred_element_type=f32)


def dot_nn(a, b):
    return lax.dot_general(a, b, (((1,), (0,)), ((), ())), preferred_element_type=f32)


def iota(shape, axis):
    return lax.broadcasted_iota(jnp.int32, shape, axis)


def pack_kernel(rows, keys, states_ref, readout_ref, out_ref):
    peers = states_ref.shape[0]
    width = states_ref.shape[2] // 2
    heads = readout_ref.shape[0]
    share = heads // KEY_VALUE_HEADS
    copies = jnp.concatenate([readout_ref[...]] * (LANES // heads), axis=0)
    group = iota((LANES, HEAD_SIZE), 0) % heads // share
    spread = jnp.concatenate(
        [jnp.where(group == g, copies, jnp.zeros_like(copies)) for g in range(KEY_VALUE_HEADS)], axis=1
    )
    body = rows * keys
    lane = iota((SUBLANES, LANES), 1)
    for p in range(peers):
        out_ref[p, :body, :] = states_ref[p, :, :width]
        read = dot_nt(states_ref[p, :, width:], spread)
        for r in range(rows):
            first = read[r * keys : r * keys + SUBLANES, :]
            second = read[r * keys + SUBLANES : r * keys + 2 * SUBLANES, :]
            value = jnp.where(lane < 2 * heads, first, second)
            high = value.astype(bf16).astype(f32)
            parts = jnp.where(lane % (2 * heads) < heads, high, value - high)
            out_ref[p, body : body + SUBLANES, r * LANES : (r + 1) * LANES] = parts.astype(bf16)


def direct_kernel(target_length, queries_ref, states_ref, readout_ref, length_ref, out_ref):
    t = pl.program_id(0)
    keys = states_ref.shape[1]
    width = states_ref.shape[2] // 2
    tokens = queries_ref.shape[1]
    slots = length_ref.shape[1]
    heads = readout_ref.shape[0]
    share = heads // KEY_VALUE_HEADS
    scale = math.log2(math.e) / math.sqrt(HEAD_SIZE)
    usable = iota((keys, share * tokens), 0) < target_length[t]
    total = jnp.zeros((1, tokens), f32)
    for g in range(KEY_VALUE_HEADS):
        k = states_ref[0, :, g * HEAD_SIZE : (g + 1) * HEAD_SIZE]
        v = states_ref[0, :, width + g * HEAD_SIZE : width + (g + 1) * HEAD_SIZE]
        q = jnp.concatenate(
            [
                queries_ref[0, :, h * HEAD_SIZE : (h + 1) * HEAD_SIZE]
                for h in range(g * share, (g + 1) * share)
            ],
            axis=0,
        )
        scores = jnp.where(usable, dot_nt(k, q), MASKED)
        weights = jnp.exp2((scores - jnp.max(scores, axis=0, keepdims=True)) * scale)
        read = dot_nt(v, readout_ref[g * share : (g + 1) * share, :])
        read = jnp.concatenate(
            [jnp.broadcast_to(read[:, h : h + 1], (keys, tokens)) for h in range(share)], axis=1
        )
        ratio = jnp.sum(weights * read, axis=0, keepdims=True) / jnp.sum(
            weights, axis=0, keepdims=True
        )
        for h in range(share):
            total = total + ratio[:, h * tokens : (h + 1) * tokens]
    source = tokens // slots
    lane = iota((slots, tokens), 1)
    length = length_ref[0]
    wanted = (lane // source == iota((slots, tokens), 0)) & (lane % source < length)
    out_ref[0] = jnp.where(wanted, jnp.broadcast_to(total, (slots, tokens)), 0.0) / length.astype(f32)


def channel_kernel(
    rows,
    place,
    row_at,
    target_length,
    arrived_ref,
    queries_ref,
    direct_ref,
    length_ref,
    row_ref,
    order_ref,
    half_order_ref,
    expand_ref,
    out_ref,
    keys_ref,
    read_ref,
):
    targets, tokens, _ = queries_ref.shape
    slots = direct_ref.shape[1]
    peers, _, width = arrived_ref.shape
    keys = keys_ref.shape[0] // slots
    body = rows * keys
    share = queries_ref.shape[2] // HEAD_SIZE // KEY_VALUE_HEADS
    columns = share * tokens
    scale = math.log2(math.e) / math.sqrt(HEAD_SIZE)
    lane = iota((slots, LANES), 1)
    gathered = jnp.zeros((slots, LANES), f32)
    position = iota((keys, slots, columns), 0)
    for t in range(targets):
        for s in range(slots):
            row = row_at[t, s]
            peer = row // rows
            r = row % rows
            keys_ref[s * keys : (s + 1) * keys, :] = arrived_ref[
                peer, pl.ds(pl.multiple_of(r * keys, keys), keys), :
            ]
            read_ref[s * SUBLANES : (s + 1) * SUBLANES, :] = arrived_ref[
                peer, body : body + SUBLANES, pl.ds(pl.multiple_of(r * LANES, LANES), LANES)
            ].astype(f32)
        key = dot_nn(order_ref[...], keys_ref[...]).astype(bf16)
        read = dot_nn(half_order_ref[...], read_ref[...].astype(bf16)).astype(bf16)
        read = dot_nn(read, expand_ref[...])
        length = jnp.concatenate([length_ref[t]] * (columns // LANES), axis=1)
        usable = position < length[None]
        total = jnp.zeros((slots, columns), f32)
        for g in range(KEY_VALUE_HEADS):
            q = jnp.concatenate(
                [
                    queries_ref[t, :, h * HEAD_SIZE : (h + 1) * HEAD_SIZE]
                    for h in range(g * share, (g + 1) * share)
                ],
                axis=0,
            )
            scores = dot_nt(key[:, g * HEAD_SIZE : (g + 1) * HEAD_SIZE], q)
            scores = jnp.where(usable, scores.reshape(keys, slots, columns), MASKED)
            weights = jnp.exp2((scores - jnp.max(scores, axis=0, keepdims=True)) * scale)
            half = KEY_VALUE_HEADS * columns
            value = jnp.concatenate(
                [
                    read[:, i * half + g * columns : i * half + (g + 1) * columns]
                    for i in range(keys // SUBLANES)
                ],
                axis=0,
            ).reshape(keys, slots, columns)
            total = total + jnp.sum(weights * value, axis=0) / jnp.sum(weights, axis=0)
        count = target_length[t]
        token = iota((slots, columns), 1) % tokens
        total = jnp.where(token < count, total, 0.0) / count.astype(f32)
        combined = direct_ref[t]
        for i in range(columns // LANES):
            combined = combined + total[:, i * LANES : (i + 1) * LANES]
        combined = jnp.sum(combined, axis=1, keepdims=True)
        gathered = gathered + jnp.where(row_ref[t] == lane, combined, 0.0)
    gathered = jnp.sum(gathered, axis=0, keepdims=True)
    at = iota((peers, LANES), 1)
    mine = iota((peers, LANES), 0) * rows
    out = jnp.zeros((peers, LANES), f32)
    for r in range(rows):
        sent = jnp.sum(jnp.where(at == mine + r, gathered, 0.0), axis=1, keepdims=True)
        out = out + jnp.where(at == place[0] * rows + r, sent, 0.0)
    out_ref[...] = out


def on_device(
    candidate_queries,
    target_states,
    target_queries,
    candidate_states,
    target_length,
    candidate_length,
    candidate_row,
    direct_readout,
    channel_readout,
    *,
    peers,
):
    targets, slots, keys, query_width = candidate_queries.shape
    tokens = target_queries.shape[1]
    candidates = candidate_states.shape[0]
    width = candidate_states.shape[2] // 2
    heads = query_width // HEAD_SIZE
    share = heads // KEY_VALUE_HEADS
    rows = candidates // peers
    columns = share * tokens
    assert keys == 2 * SUBLANES and slots == SUBLANES
    assert 4 * heads == LANES and slots * keys == LANES
    assert rows * LANES <= width and candidates <= LANES

    body = rows * keys
    chunk = body + SUBLANES
    step = max(1, peers // 4)
    packed = pl.pallas_call(
        functools.partial(pack_kernel, rows, keys),
        out_shape=jax.ShapeDtypeStruct((peers, chunk, width), bf16),
        grid=(peers // step,),
        in_specs=[
            pl.BlockSpec((step, body, 2 * width), lambda i: (i, 0, 0)),
            pl.BlockSpec((heads, HEAD_SIZE), lambda i: (0, 0)),
        ],
        out_specs=pl.BlockSpec((step, chunk, width), lambda i: (i, 0, 0)),
        compiler_params=pltpu.CompilerParams(vmem_limit_bytes=16 * 2**20),
        name="pack",
    )(
        candidate_states.reshape(peers, body, 2 * width),
        channel_readout.reshape(heads, HEAD_SIZE),
    )
    arrived = lax.all_to_all(packed, "dp", split_axis=0, concat_axis=0, tiled=True)

    length_lanes = jnp.broadcast_to(candidate_length[:, :, None], (targets, slots, LANES))
    row_lanes = jnp.broadcast_to(candidate_row[:, :, None], (targets, slots, LANES))
    direct = pl.pallas_call(
        direct_kernel,
        out_shape=jax.ShapeDtypeStruct((targets, slots, slots * keys), f32),
        grid_spec=pltpu.PrefetchScalarGridSpec(
            num_scalar_prefetch=1,
            grid=(targets,),
            in_specs=[
                pl.BlockSpec((1, slots * keys, query_width), lambda t, n: (t, 0, 0)),
                pl.BlockSpec((1, tokens, 2 * width), lambda t, n: (t, 0, 0)),
                pl.BlockSpec((heads, HEAD_SIZE), lambda t, n: (0, 0)),
                pl.BlockSpec((1, slots, LANES), lambda t, n: (t, 0, 0)),
            ],
            out_specs=pl.BlockSpec((1, slots, slots * keys), lambda t, n: (t, 0, 0)),
        ),
        compiler_params=pltpu.CompilerParams(vmem_limit_bytes=32 * 2**20),
        cost_estimate=pl.CostEstimate(
            flops=4 * candidate_queries.size * tokens,
            bytes_accessed=2 * candidate_queries.size,
            transcendentals=0,
        ),
        name="direct",
    )(
        target_length,
        candidate_queries.reshape(targets, slots * keys, query_width),
        target_states,
        direct_readout.reshape(heads, HEAD_SIZE),
        length_lanes,
    )

    pairs = slots * keys
    to = jnp.arange(pairs, dtype=jnp.int32)[:, None]
    come = jnp.arange(pairs, dtype=jnp.int32)[None, :]
    order = ((to % slots == come // keys) & (to // slots == come % keys)).astype(bf16)
    to, come = to[: pairs // 2], come[:, : pairs // 2]
    half_order = ((to % slots == come // SUBLANES) & (to // slots == come % SUBLANES)).astype(bf16)
    value = jnp.arange(LANES, dtype=jnp.int32)[:, None]
    column = jnp.arange(2 * heads * tokens, dtype=jnp.int32)[None, :]
    expand = (
        (value // (2 * heads) == column // (heads * tokens))
        & (value % heads == column // tokens % heads)
    ).astype(bf16)

    place = lax.axis_index("dp").astype(jnp.int32).reshape(1)
    vmem = pl.BlockSpec(memory_space=pltpu.VMEM)
    smem = pl.BlockSpec(memory_space=pltpu.SMEM)
    outgoing = pl.pallas_call(
        functools.partial(channel_kernel, rows),
        out_shape=jax.ShapeDtypeStruct((peers, LANES), f32),
        in_specs=[smem] * 3 + [vmem] * 8,
        out_specs=vmem,
        scratch_shapes=[
            pltpu.VMEM((slots * keys, width), bf16),
            pltpu.VMEM((slots * SUBLANES, LANES), f32),
        ],
        compiler_params=pltpu.CompilerParams(vmem_limit_bytes=32 * 2**20),
        name="channel",
    )(
        place,
        candidate_row,
        target_length,
        arrived,
        target_queries,
        direct,
        length_lanes,
        row_lanes,
        order,
        half_order,
        expand,
    )
    returned = lax.all_to_all(outgoing, "dp", split_axis=0, concat_axis=0, tiled=True)
    return jnp.sum(returned, axis=0)[:candidates]


def solution(mesh):
    in_specs = (
        P(("group", "dp"), None, None, None),
        P(("group", "dp"), None, None),
        P(("group", "dp"), None, None),
        P(("group", "dp"), None, None),
        P(("group", "dp")),
        P(("group", "dp"), None),
        P(("group", "dp"), None),
        P(),
        P(),
    )
    out_specs = P(("group", "dp"))
    return jax.shard_map(
        functools.partial(on_device, peers=mesh.shape["dp"]),
        mesh=mesh,
        in_specs=in_specs,
        out_specs=out_specs,
        check_vma=False,
    )
```

time: 183 us -> 57.3 us (0.31)
  local copies, waits for them, and re-layouts: 88.3 us -> 7.92 us
  matrix products: 67.8 us -> 0 us
  waiting for transfers between devices: 0.01 us -> 13.9 us
  Pallas kernels: 0 us -> 12.1 us
  other arithmetic: 5.21 us -> 1.81 us
    dot_general x5 -> x0, matrix products: 52.1 us -> none  [the longest x2 27.6 us: pooled(): tokens = jnp.dot(mixture, readout, preferred_element_type=jnp.float32)]
    convert_element_type x2 -> x0, local copies, waits for them, and re-layouts: 29.6 us -> none  [the longest x1 17.5 us: attend_paired(): mixture.astype(jnp.bfloat16)]
    reshape x3 -> x0, local copies, waits for them, and re-layouts: 25.8 us -> none  [the longest x1 25.3 us: attend_paired(): mixture.astype(jnp.bfloat16)]
    sub x1 -> x0, matrix products: 15.7 us -> none  [softmax_weights(): weights = jnp.exp(scores - highest)]
    all_to_all x1, waiting for transfers between devices: 0.01 us -> 13.9 us  [on_device(): lax.all_to_all(packed, 'dp', split_axis=0, concat_axis=0, tiled=True)]
    another operation x1 -> x0, local copies, waits for them, and re-layouts: 13.3 us -> none  [on_device(): direct_mix.reshape(target_count, slot_count, source_length, model_width)]
    pallas_call x0 -> x3, Pallas kernels: none -> 12.1 us  [the longest x1 5.35 us: on_device(): pl.pallas_call(direct_kernel, out_shape=jax.ShapeDtypeStruct((targets, sl...]
    gather x2 -> x0, local copies, waits for them, and re-layouts: 5.26 us -> none  [on_device(): jnp.take(arrived, flat_rows, axis=0)]
  transfers between devices with their start and end apart: 1 -> 1, of which waited for: 0 -> 1; matrix products, arithmetic and copies ran while one was open for 36% -> 2% of each run, Pallas kernels for 0% -> 9%
where the time goes in v1:
time: 57.3 us; the launch traced here: 56.9 us
  waiting for transfers between devices  13.9 us (24%)
  blocking collectives  13.7 us (24%)
  Pallas kernels  12.1 us (21%)
  local copies, waits for them, and re-layouts  7.92 us (14%)
  starting transfers between devices  7.4 us (13%)
  other arithmetic  1.81 us (3%)
    all_to_all x1, waiting for transfers between devices, on_device(): lax.all_to_all(packed, 'dp', split_axis=0, concat_axis=0, tiled=True)  13.9 us
    all_to_all x1, blocking collectives, on_device(): lax.all_to_all(outgoing, 'dp', split_axis=0, concat_axis=0, tiled=True)  13.7 us
    unnamed x20, local copies, waits for them, and re-layouts  7.77 us
    all_to_all x1, starting transfers between devices, on_device(): lax.all_to_all(packed, 'dp', split_axis=0, concat_axis=0, tiled=True)  7.4 us
    pallas_call x1, Pallas kernels, on_device(): pl.pallas_call(direct_kernel, out_shape=jax.ShapeDtypeStruct((targets, sl...  5.35 us
    pallas_call x1, Pallas kernels, on_device(): pl.pallas_call(functools.partial(channel_kernel, rows), out_shape=jax.Sha...  4.39 us
    pallas_call x1, Pallas kernels, on_device(): pl.pallas_call(functools.partial(pack_kernel, rows, keys), out_shape=jax....  2.34 us
  transfers between devices with their start and end apart: 1, of which 1 were waited for; matrix products, arithmetic and copies ran while one was open for 2% of the time, Pallas kernels for 9%

profile of v1, /device:TPU:0, one launch (start us, length us, event | category | flops | bytes accessed | tf_op | source)
XLA Modules:
  0.0 56.9 jit_solution(16288379530540281181)
XLA Ops:
  0.0 0.0 copy-start.3
  0.0 1.6 %copy-done.3 = bf16[64,16,1024]{2,1,0:T(8,128)(2,1)S(1)} copy-done((bf16[64,16,1024]{2,1,0:T(8,128)(2,1)S(1)}, bf16[64,16,1024]{2,1,0:T(8,128)(2,1)}, u32[]{:S(2)}) %copy-start.3) | copy-done | bytes 2097176
  1.6 0.0 copy-start.6
  1.6 0.7 %copy-done.6 = bf16[4096]{0:T(1024)(128)(2,1)S(1)} copy-done((bf16[4096]{0:T(1024)(128)(2,1)S(1)}, bf16[4096]{0:T(1024)(128)(2,1)}, u32[]{:S(2)}) %copy-start.6) | copy-done | bytes 8216
  2.3 2.3 %pack.1 = bf16[16,72,512]{2,1,0:T(8,128)(2,1)} custom-call(bf16[16,64,1024]{2,1,0:T(8,128)(2,1)S(1)} %bitcast.18, bf16[32,128]{1,0:T(8,128)(2,1)S(1)} %bitcast.20), custom_call_target="tpu_custom_call" | custom-call | tf_op jit(solution)/shard_map/pack/pallas_call | solution.py:207
  4.6 7.4 %all-to-all-start = ((bf16[16,72,512]{2,1,0:T(8,128)(2,1)}), bf16[16,72,512]{2,1,0:T(8,128)(2,1)S(1)}, u32[]{:S(2)}, u32[]{:S(2)}) async-start(bf16[16,72,512]{2,1,0:T(8,128)(2,1)} %pack.1), calls=%async_computation | async-start | bytes 2359296 | tf_op jit(solution)/shard_map/all_to_all | solution.py:222
  12.1 0.0 copy-done.9
  12.1 0.1 broadcast_in_dim.4.length_ref
  12.1 0.0 copy-done.7
  12.1 0.0 copy-done.8
  12.2 3.4 %copy-done = bf16[8,8,16,4096]{3,2,1,0:T(8,128)(2,1)S(1)} copy-done((bf16[8,8,16,4096]{3,2,1,0:T(8,128)(2,1)S(1)}, bf16[8,8,16,4096]{3,2,1,0:T(8,128)(2,1)}, u32[]{:S(2)}) %copy-start) | copy-done | bytes 8388632
  15.5 1.0 %copy-done.4 = bf16[8,32,1024]{2,1,0:T(8,128)(2,1)S(1)} copy-done((bf16[8,32,1024]{2,1,0:T(8,128)(2,1)S(1)}, bf16[8,32,1024]{2,1,0:T(8,128)(2,1)}, u32[]{:S(2)}) %copy-start.4) | copy-done | bytes 524312
  16.6 5.4 %direct.1.direct_ref = f32[8,8,128]{2,1,0:T(8,128)S(1)} custom-call(s32[8]{0:T(128)S(1)} %copy-done.8, bf16[8,128,4096]{2,1,0:T(8,128)(2,1)S(1)} %bitcast.17, bf16[8,32,1024]{2,1,0:T(8,128)(2,1)S(1)} %copy-done.4, bf16[32,128]{1,0:T(8,128)(2,1)S(1)} %bitcast.21, s32[8,8,128]{2,1,0:T(8,128)S(1)} %broadcast_in_dim.4.length_ref), custom_call_target="tpu_custom_call" | custom-call | flops 536870912 | bytes 8388608 | tf_op jit(solution)/shard_map/direct/pallas_call | solution.py:226
  22.1 0.1 and_convert_fusion.2.half_order_ref
  22.1 0.1 and_convert_fusion.1.order_ref
  22.2 1.0 %and_convert_fusion.expand_ref = bf16[128,2048]{1,0:T(8,128)(2,1)} fusion(s32[2048]{0:T(1024)S(1)} %get-tuple-element.13, s32[2048]{0:T(1024)S(1)} %get-tuple-element.14, s32[128]{0:T(128)S(1)} %get-tuple-element.15, s32[128]{0:T(128)S(1)} %get-tuple-element.16), kind=kLoop, calls=%fused_computation | loop fusion | flops 1048576 | bytes 541696 | tf_op jit(solution)/shard_map/convert_element_type | solution.py:266
  23.3 13.9 %all-to-all-done.arrived_ref = bf16[16,72,512]{2,1,0:T(8,128)(2,1)S(1)} async-done(((bf16[16,72,512]{2,1,0:T(8,128)(2,1)}), bf16[16,72,512]{2,1,0:T(8,128)(2,1)S(1)}, u32[]{:S(2)}, u32[]{:S(2)}) %all-to-all-start) | async-done | bytes 1179680 | tf_op jit(solution)/shard_map/all_to_all | solution.py:222
  37.2 0.0 copy-done.5
  37.2 0.1 broadcast_in_dim.5.row_ref
  37.2 0.0 copy-done.1
  37.3 1.0 %copy-done.2 = bf16[128,2048]{1,0:T(8,128)(2,1)S(1)} copy-done((bf16[128,2048]{1,0:T(8,128)(2,1)S(1)}, bf16[128,2048]{1,0:T(8,128)(2,1)}, u32[]{:S(2)}) %copy-start.2) | copy-done | bytes 524312
  38.3 4.4 %channel.1 = f32[16,128]{1,0:T(8,128)S(1)} custom-call(s32[1]{0:T(128)} %bitcast.place, s32[8,8]{1,0:T(8,128)S(1)} %copy-done.5, s32[8]{0:T(128)S(1)} %copy-done.8, bf16[16,72,512]{2,1,0:T(8,128)(2,1)S(1)} %all-to-all-done.arrived_ref, bf16[8,32,4096]{2,1,0:T(8,128)(2,1)S(1)} %copy-done.1, f32[8,8,128]{2,1,0:T(8,128)S(1)} %direct.1.direct_ref, ...), custom_call_target="tpu_custom_call" | custom-call | tf_op jit(solution)/shard_map/channel/pallas_call | solution.py:271
  42.7 13.7 %all_to_all.14 = f32[16,1,128]{2,1,0:T(1,128)S(1)} all-to-all(f32[16,1,128]{2,1,0:T(1,128)S(1)} %bitcast.19), channel_id=1, replica_groups=mesh['group'=2,'dp'=16] {'dp'}, dimensions={0} | all-to-all | bytes 16384 | tf_op jit(solution)/shard_map/all_to_all | solution.py:295
  56.4 0.5 reduce_sum.9
  (18 shorter events, 0.1 us)
Async XLA Ops:
  0.0 1.6 %copy-start.3 = (bf16[64,16,1024]{2,1,0:T(8,128)(2,1)S(1)}, bf16[64,16,1024]{2,1,0:T(8,128)(2,1)}, u32[]{:S(2)}) copy-start(bf16[64,16,1024]{2,1,0:T(8,128)(2,1)} %param.12) | copy-start | bytes 6291460
  1.6 0.7 %copy-start.6 = (bf16[4096]{0:T(1024)(128)(2,1)S(1)}, bf16[4096]{0:T(1024)(128)(2,1)}, u32[]{:S(2)}) copy-start(bf16[4096]{0:T(1024)(128)(2,1)} %param.17) | copy-start | bytes 24580
  2.3 9.8 %copy-start.9 = (s32[8,8]{1,0:T(8,128)S(1)}, s32[8,8]{1,0:T(8,128)}, u32[]{:S(2)}) copy-start(s32[8,8]{1,0:T(8,128)} %param.14) | copy-start | bytes 772
  2.3 9.8 %copy-start.7 = (bf16[4096]{0:T(1024)(128)(2,1)S(1)}, bf16[4096]{0:T(1024)(128)(2,1)}, u32[]{:S(2)}) copy-start(bf16[4096]{0:T(1024)(128)(2,1)} %param.16) | copy-start | bytes 24580
  2.3 9.8 %copy-start.8 = (s32[8]{0:T(128)S(1)}, s32[8]{0:T(128)}, u32[]{:S(2)}) copy-start(s32[8]{0:T(128)} %target_length.3) | copy-start | bytes 100
  4.6 32.5 %all-to-all-start = ((bf16[16,72,512]{2,1,0:T(8,128)(2,1)}), bf16[16,72,512]{2,1,0:T(8,128)(2,1)S(1)}, u32[]{:S(2)}, u32[]{:S(2)}) async-start(bf16[16,72,512]{2,1,0:T(8,128)(2,1)} %pack.1), calls=%async_computation | async-start | bytes 2359296 | tf_op jit(solution)/shard_map/all_to_all | solution.py:222
  12.1 3.4 %copy-start = (bf16[8,8,16,4096]{3,2,1,0:T(8,128)(2,1)S(1)}, bf16[8,8,16,4096]{3,2,1,0:T(8,128)(2,1)}, u32[]{:S(2)}) copy-start(bf16[8,8,16,4096]{3,2,1,0:T(8,128)(2,1)} %param.9) | copy-start | bytes 25165828
  15.5 1.0 %copy-start.4 = (bf16[8,32,1024]{2,1,0:T(8,128)(2,1)S(1)}, bf16[8,32,1024]{2,1,0:T(8,128)(2,1)}, u32[]{:S(2)}) copy-start(bf16[8,32,1024]{2,1,0:T(8,128)(2,1)} %states_ref.1) | copy-start | bytes 1572868
  16.6 20.6 %copy-start.5 = (s32[8,8]{1,0:T(8,128)S(1)}, s32[8,8]{1,0:T(8,128)}, u32[]{:S(2)}) copy-start(s32[8,8]{1,0:T(8,128)} %row_at.1) | copy-start | bytes 772
  16.6 20.7 %copy-start.1 = (bf16[8,32,4096]{2,1,0:T(8,128)(2,1)S(1)}, bf16[8,32,4096]{2,1,0:T(8,128)(2,1)}, u32[]{:S(2)}) copy-start(bf16[8,32,4096]{2,1,0:T(8,128)(2,1)} %queries_ref.1) | copy-start | bytes 6291460
  37.2 1.0 %copy-start.2 = (bf16[128,2048]{1,0:T(8,128)(2,1)S(1)}, bf16[128,2048]{1,0:T(8,128)(2,1)}, u32[]{:S(2)}) copy-start(bf16[128,2048]{1,0:T(8,128)(2,1)} %and_convert_fusion.expand_ref) | copy-start | bytes 1572868

commit v2 on v1

v2 whole, which is shorter than its diff:
```python
import functools
import math

import jax
import jax.numpy as jnp
from jax import lax
from jax.experimental import pallas as pl
from jax.experimental.pallas import tpu as pltpu
from jax.sharding import PartitionSpec as P

KEY_VALUE_HEADS = 4
HEAD_SIZE = 128
LANES = 128
SUBLANES = 8
MASKED = -1e30
PACK_LIMIT = 60 * 2**20

bf16 = jnp.bfloat16
f32 = jnp.float32


def dot_nt(a, b):
    return lax.dot_general(a, b, (((1,), (1,)), ((), ())), preferred_element_type=f32)


def dot_nn(a, b):
    return lax.dot_general(a, b, (((1,), (0,)), ((), ())), preferred_element_type=f32)


def iota(shape, axis):
    return lax.broadcasted_iota(jnp.int32, shape, axis)


def pack_kernel(rows, keys, states_ref, readout_ref, out_ref, values_ref, read_ref, sent_ref, sems):
    peers, body, width = values_ref.shape
    half = width // 2
    heads = read_ref.shape[0]
    share = heads // KEY_VALUE_HEADS
    parts = (sems.shape[0] - 1) // 4
    step = peers // parts
    load_readout = pltpu.make_async_copy(readout_ref, read_ref, sems.at[0])
    load_readout.start()
    loads, moves, sends = [], [], []
    for i in range(parts):
        at = pl.ds(i * step, step)
        loads.append(
            pltpu.make_async_copy(
                states_ref.at[at, :, width:], values_ref.at[at], sems.at[1 + i]
            )
        )
        loads[i].start()
    for i in range(parts):
        at = pl.ds(i * step, step)
        for j in range(2):
            moves.append(
                pltpu.make_async_copy(
                    states_ref.at[at, :, j * half : (j + 1) * half],
                    sent_ref.at[at, j * body : (j + 1) * body, :],
                    sems.at[1 + (1 + j) * parts + i],
                )
            )
            moves[-1].start()
    load_readout.wait()
    repeated = jnp.concatenate([read_ref[...]] * (LANES // heads), axis=0)
    group = iota((LANES, HEAD_SIZE), 0) % heads // share
    spread = jnp.concatenate(
        [jnp.where(group == g, repeated, jnp.zeros_like(repeated)) for g in range(KEY_VALUE_HEADS)],
        axis=1,
    )
    lane = iota((keys, LANES), 1)
    for i in range(parts):
        loads[i].wait()
        read = dot_nt(values_ref[i * step : (i + 1) * step].reshape(step * body, width), spread)
        for p in range(step):
            for j in range(half // LANES):
                even = min(2 * j, rows - 1)
                odd = min(2 * j + 1, rows - 1)
                even = read[p * body + even * keys : p * body + (even + 1) * keys, :]
                odd = read[p * body + odd * keys : p * body + (odd + 1) * keys, :]
                value = jnp.where(lane < 2 * heads, even, odd)
                high = value.astype(bf16).astype(f32)
                value = jnp.where(lane % (2 * heads) < heads, high, value - high)
                sent_ref[i * step + p, 2 * body :, j * LANES : (j + 1) * LANES] = value.astype(bf16)
        moves[2 * i].wait()
        moves[2 * i + 1].wait()
        at = pl.ds(i * step, step)
        sends.append(
            pltpu.make_async_copy(sent_ref.at[at], out_ref.at[at], sems.at[1 + 3 * parts + i])
        )
        sends[i].start()
    for copy in sends:
        copy.wait()


def direct_kernel(target_length, queries_ref, states_ref, readout_ref, length_ref, out_ref):
    t = pl.program_id(0)
    keys = states_ref.shape[1]
    width = states_ref.shape[2] // 2
    tokens = queries_ref.shape[1]
    slots = length_ref.shape[1]
    heads = readout_ref.shape[0]
    share = heads // KEY_VALUE_HEADS
    scale = math.log2(math.e) / math.sqrt(HEAD_SIZE)
    usable = iota((keys, share * tokens), 0) < target_length[t]
    total = jnp.zeros((1, tokens), f32)
    for g in range(KEY_VALUE_HEADS):
        k = states_ref[0, :, g * HEAD_SIZE : (g + 1) * HEAD_SIZE]
        v = states_ref[0, :, width + g * HEAD_SIZE : width + (g + 1) * HEAD_SIZE]
        q = jnp.concatenate(
            [
                queries_ref[0, :, h * HEAD_SIZE : (h + 1) * HEAD_SIZE]
                for h in range(g * share, (g + 1) * share)
            ],
            axis=0,
        )
        scores = jnp.where(usable, dot_nt(k, q), MASKED)
        weights = jnp.exp2((scores - jnp.max(scores, axis=0, keepdims=True)) * scale)
        read = dot_nt(v, readout_ref[g * share : (g + 1) * share, :])
        read = jnp.concatenate(
            [jnp.broadcast_to(read[:, h : h + 1], (keys, tokens)) for h in range(share)], axis=1
        )
        ratio = jnp.sum(weights * read, axis=0, keepdims=True) / jnp.sum(
            weights, axis=0, keepdims=True
        )
        for h in range(share):
            total = total + ratio[:, h * tokens : (h + 1) * tokens]
    source = tokens // slots
    lane = iota((slots, tokens), 1)
    length = length_ref[0]
    wanted = (lane // source == iota((slots, tokens), 0)) & (lane % source < length)
    out_ref[0] = jnp.where(wanted, jnp.broadcast_to(total, (slots, tokens)), 0.0) / length.astype(f32)


def channel_kernel(
    rows,
    share,
    at_ref,
    arrived_ref,
    queries_ref,
    direct_ref,
    length_ref,
    row_ref,
    pick_ref,
    weight_ref,
    mine_ref,
    out_ref,
    keys_ref,
    read_ref,
):
    targets = queries_ref.shape[0]
    columns = queries_ref.shape[3]
    slots = direct_ref.shape[1]
    peers = out_ref.shape[0]
    keys = keys_ref.shape[2] // slots
    body = rows * keys
    heads = KEY_VALUE_HEADS * share
    per = arrived_ref.shape[1] // HEAD_SIZE
    scale = math.log2(math.e) / math.sqrt(HEAD_SIZE)
    lane = iota((slots, LANES), 1)
    position = iota((keys, slots, columns), 0)
    gathered = jnp.zeros((slots, LANES), f32)
    for t in range(targets):
        for s in range(slots):
            start = pl.multiple_of(at_ref[0, t * slots + s], keys)
            for j in range(KEY_VALUE_HEADS // per):
                key = arrived_ref[pl.ds(start + j * body, keys), :].astype(f32)
                for g in range(per):
                    keys_ref[t, j * per + g, pl.ds(s, keys, stride=slots), :] = key[
                        :, g * HEAD_SIZE : (g + 1) * HEAD_SIZE
                    ]
            start = pl.multiple_of(at_ref[1, t * slots + s], keys)
            across = pl.multiple_of(at_ref[2, t * slots + s], LANES)
            read_ref[t, pl.ds(s, keys, stride=slots), :] = arrived_ref[
                pl.ds(start, keys), pl.ds(across, LANES)
            ].astype(f32)
        read = read_ref[t]
        read = read + pltpu.roll(read, LANES - heads, 1)
        usable = position < jnp.concatenate([length_ref[t]] * (columns // LANES), axis=1)[None]
        total = jnp.zeros((slots, columns), f32)
        for g in range(KEY_VALUE_HEADS):
            scores = dot_nn(keys_ref[t, g].astype(bf16), queries_ref[t, g])
            scores = jnp.where(usable, scores.reshape(keys, slots, columns), MASKED)
            weights = jnp.exp2((scores - jnp.max(scores, axis=0, keepdims=True)) * scale)
            pick = pick_ref[t] + g * share
            value = jnp.concatenate(
                [
                    jnp.take_along_axis(read[i * slots : (i + 1) * slots, :], pick, axis=1)
                    for i in range(keys)
                ],
                axis=0,
            )
            value = jnp.concatenate([value] * (columns // LANES), axis=1)
            value = value.reshape(keys, slots, columns)
            total = total + jnp.sum(weights * value, axis=0) / jnp.sum(weights, axis=0)
        total = total * weight_ref[t : t + 1, :]
        combined = direct_ref[t]
        for i in range(columns // LANES):
            combined = combined + total[:, i * LANES : (i + 1) * LANES]
        combined = jnp.sum(combined, axis=1, keepdims=True)
        gathered = gathered + jnp.where(row_ref[t] == lane, combined, 0.0)
    gathered = jnp.sum(gathered, axis=0, keepdims=True)
    at = iota((peers, LANES), 1) - iota((peers, LANES), 0) * rows
    out = jnp.zeros((peers, LANES), f32)
    for r in range(rows):
        sent = jnp.sum(jnp.where(at == r, gathered, 0.0), axis=1, keepdims=True)
        out = out + jnp.where(mine_ref[...] == r, sent, 0.0)
    out_ref[...] = out


def on_device(
    candidate_queries,
    target_states,
    target_queries,
    candidate_states,
    target_length,
    candidate_length,
    candidate_row,
    direct_readout,
    channel_readout,
    *,
    peers,
):
    targets, slots, keys, query_width = candidate_queries.shape
    tokens = target_queries.shape[1]
    candidates = candidate_states.shape[0]
    width = candidate_states.shape[2] // 2
    heads = query_width // HEAD_SIZE
    share = heads // KEY_VALUE_HEADS
    rows = candidates // peers
    columns = share * tokens
    assert slots == SUBLANES and keys == 2 * SUBLANES and slots * keys == LANES
    assert 4 * heads == LANES and width == 4 * LANES and rows <= 4 and candidates <= LANES

    body = rows * keys
    chunk = 2 * body + keys
    parts = 4
    hbm = pl.BlockSpec(memory_space=pltpu.HBM)
    packed = pl.pallas_call(
        functools.partial(pack_kernel, rows, keys),
        out_shape=jax.ShapeDtypeStruct((peers, chunk, width // 2), bf16),
        in_specs=[hbm, hbm],
        out_specs=hbm,
        scratch_shapes=[
            pltpu.VMEM((peers, body, width), bf16),
            pltpu.VMEM((heads, HEAD_SIZE), bf16),
            pltpu.VMEM((peers, chunk, width // 2), bf16),
            pltpu.SemaphoreType.DMA((1 + 4 * parts,)),
        ],
        compiler_params=pltpu.CompilerParams(vmem_limit_bytes=PACK_LIMIT),
        name="pack",
    )(
        candidate_states.reshape(peers, body, 2 * width),
        channel_readout.reshape(heads, HEAD_SIZE),
    )
    arrived = lax.all_to_all(packed, "dp", split_axis=0, concat_axis=0, tiled=True)

    length_lanes = jnp.broadcast_to(candidate_length[:, :, None], (targets, slots, LANES))
    row_lanes = jnp.broadcast_to(candidate_row[:, :, None], (targets, slots, LANES))
    direct = pl.pallas_call(
        direct_kernel,
        out_shape=jax.ShapeDtypeStruct((targets, slots, slots * keys), f32),
        grid_spec=pltpu.PrefetchScalarGridSpec(
            num_scalar_prefetch=1,
            grid=(targets,),
            in_specs=[
                pl.BlockSpec((1, slots * keys, query_width), lambda t, n: (t, 0, 0)),
                pl.BlockSpec((1, tokens, 2 * width), lambda t, n: (t, 0, 0)),
                pl.BlockSpec((heads, HEAD_SIZE), lambda t, n: (0, 0)),
                pl.BlockSpec((1, slots, LANES), lambda t, n: (t, 0, 0)),
            ],
            out_specs=pl.BlockSpec((1, slots, slots * keys), lambda t, n: (t, 0, 0)),
        ),
        compiler_params=pltpu.CompilerParams(vmem_limit_bytes=32 * 2**20),
        cost_estimate=pl.CostEstimate(
            flops=4 * candidate_queries.size * tokens,
            bytes_accessed=2 * candidate_queries.size,
            transcendentals=0,
        ),
        name="direct",
    )(
        target_length,
        candidate_queries.reshape(targets, slots * keys, query_width),
        target_states,
        direct_readout.reshape(heads, HEAD_SIZE),
        length_lanes,
    )

    queries = target_queries.reshape(targets, tokens, KEY_VALUE_HEADS, share, HEAD_SIZE)
    queries = queries.transpose(0, 2, 4, 1, 3).reshape(
        targets, KEY_VALUE_HEADS, HEAD_SIZE, columns
    )
    flat = candidate_row.reshape(candidates)
    at = jnp.stack(
        [
            flat // rows * chunk + flat % rows * keys,
            flat // rows * chunk + 2 * body,
            flat % rows // 2 * LANES,
        ]
    )
    lanes = jnp.arange(LANES, dtype=jnp.int32)
    pick = lanes % share + row_lanes % rows % 2 * (2 * heads)
    token = jnp.arange(columns, dtype=jnp.int32)[None, :] // share
    count = target_length[:, None]
    weight = jnp.where(token < count, 1.0 / count.astype(f32), 0.0)
    mine = (lanes - lax.axis_index("dp").astype(jnp.int32) * rows)[None, :]
    vmem = pl.BlockSpec(memory_space=pltpu.VMEM)
    smem = pl.BlockSpec(memory_space=pltpu.SMEM)
    outgoing = pl.pallas_call(
        functools.partial(channel_kernel, rows, share),
        out_shape=jax.ShapeDtypeStruct((peers, LANES), f32),
        in_specs=[smem] + [vmem] * 8,
        out_specs=vmem,
        scratch_shapes=[
            pltpu.VMEM((targets, KEY_VALUE_HEADS, slots * keys, HEAD_SIZE), f32),
            pltpu.VMEM((targets, slots * keys, LANES), f32),
        ],
        compiler_params=pltpu.CompilerParams(vmem_limit_bytes=32 * 2**20),
        name="channel",
    )(
        at,
        arrived.reshape(peers * chunk, width // 2),
        queries,
        direct,
        length_lanes,
        row_lanes,
        pick,
        weight,
        mine,
    )
    returned = lax.all_to_all(outgoing, "dp", split_axis=0, concat_axis=0, tiled=True)
    return jnp.sum(returned, axis=0)[:candidates]


def solution(mesh):
    in_specs = (
        P(("group", "dp"), None, None, None),
        P(("group", "dp"), None, None),
        P(("group", "dp"), None, None),
        P(("group", "dp"), None, None),
        P(("group", "dp")),
        P(("group", "dp"), None),
        P(("group", "dp"), None),
        P(),
        P(),
    )
    out_specs = P(("group", "dp"))
    return jax.shard_map(
        functools.partial(on_device, peers=mesh.shape["dp"]),
        mesh=mesh,
        in_specs=in_specs,
        out_specs=out_specs,
        check_vma=False,
    )
```

time: 57.3 us -> 53.2 us (0.928)
  waiting for transfers between devices: 13.9 us -> 7.98 us
  local copies, waits for them, and re-layouts: 7.92 us -> 11.5 us
  other arithmetic: 1.81 us -> 0.79 us
  Pallas kernels: 12.1 us -> 11.3 us
    all_to_all x1, waiting for transfers between devices: 13.9 us -> 7.98 us  [on_device(): lax.all_to_all(packed, 'dp', split_axis=0, concat_axis=0, tiled=True)]
    reshape x0 -> x2, local copies, waits for them, and re-layouts: none -> 2.97 us  [the longest x1 2.89 us: on_device(): queries.transpose(0, 2, 4, 1, 3)]
    transpose x0 -> x1, local copies, waits for them, and re-layouts: none -> 1.89 us  [on_device(): queries.transpose(0, 2, 4, 1, 3)]
    pallas_call x1, Pallas kernels: 4.39 us -> 2.89 us  [on_device(): pl.pallas_call(functools.partial(channel_kernel, rows, share), out_shape=...]
    unnamed x20 -> x13, local copies, waits for them, and re-layouts: 7.77 us -> 6.51 us
    convert_element_type x3 -> x0, other arithmetic: 1.21 us -> none  [the longest x1 1.03 us: on_device(): expand = ((value // (2 * heads) == column // (heads * tokens)) & (value %...]
    pallas_call x1, Pallas kernels: 2.34 us -> 3.05 us  [on_device(): pl.pallas_call(functools.partial(pack_kernel, rows, keys), out_shape=jax....]
  transfers between devices with their start and end apart: 1 -> 1, of which waited for: 1 -> 1; matrix products, arithmetic and copies ran while one was open for 2% -> 14% of each run, Pallas kernels for 9% -> 10%
where the time goes in v2:
time: 53.2 us; the launch traced here: 52.8 us
  blocking collectives  13.7 us (26%)
  local copies, waits for them, and re-layouts  11.5 us (22%)
  Pallas kernels  11.3 us (21%)
  waiting for transfers between devices  7.98 us (15%)
  starting transfers between devices  7.4 us (14%)
  other arithmetic  0.79 us (1%)
    all_to_all x1, blocking collectives, on_device(): lax.all_to_all(outgoing, 'dp', split_axis=0, concat_axis=0, tiled=True)  13.7 us
    all_to_all x1, waiting for transfers between devices, on_device(): lax.all_to_all(packed, 'dp', split_axis=0, concat_axis=0, tiled=True)  7.98 us
    all_to_all x1, starting transfers between devices, on_device(): lax.all_to_all(packed, 'dp', split_axis=0, concat_axis=0, tiled=True)  7.4 us
    unnamed x13, local copies, waits for them, and re-layouts  6.51 us
    pallas_call x1, Pallas kernels, on_device(): pl.pallas_call(direct_kernel, out_shape=jax.ShapeDtypeStruct((targets, sl...  5.35 us
    pallas_call x1, Pallas kernels, on_device(): pl.pallas_call(functools.partial(pack_kernel, rows, keys), out_shape=jax....  3.05 us
    reshape x1, local copies, waits for them, and re-layouts, on_device(): queries.transpose(0, 2, 4, 1, 3)  2.89 us
    pallas_call x1, Pallas kernels, on_device(): pl.pallas_call(functools.partial(channel_kernel, rows, share), out_shape=...  2.89 us
  transfers between devices with their start and end apart: 1, of which 1 were waited for; matrix products, arithmetic and copies ran while one was open for 14% of the time, Pallas kernels for 10%

profile of v2, /device:TPU:0, one launch (start us, length us, event | category | flops | bytes accessed | tf_op | source)
XLA Modules:
  0.0 52.8 jit_solution(3380441402005278838)
XLA Ops:
  0.0 0.0 copy-start.4
  0.0 3.1 %pack.1 = bf16[16,144,256]{2,1,0:T(8,128)(2,1)} custom-call(bf16[16,64,1024]{2,1,0:T(8,128)(2,1)} %bitcast.24, bf16[32,128]{1,0:T(8,128)(2,1)} %bitcast.26), custom_call_target="tpu_custom_call" | custom-call | tf_op jit(solution)/shard_map/pack/pallas_call | solution.py:238
  3.1 7.4 %all-to-all-start = ((bf16[16,144,256]{2,1,0:T(8,128)(2,1)}), bf16[16,144,256]{2,1,0:T(8,128)(2,1)S(1)}, u32[]{:S(2)}, u32[]{:S(2)}) async-start(bf16[16,144,256]{2,1,0:T(8,128)(2,1)} %pack.1), calls=%async_computation | async-start | bytes 2359296 | tf_op jit(solution)/shard_map/all_to_all | solution.py:255
  10.5 0.0 copy-done.4
  10.5 0.1 reshape.263
  10.6 2.1 %copy.17 = bf16[32,8,32,128]{3,2,1,0:T(8,128)(2,1)S(1)} copy(bf16[32,8,32,128]{3,1,2,0:T(8,128)(2,1)} %bitcast.25) | data formatting | bytes 4194304
  12.6 1.9 %copy.19 = bf16[8,4,128,32,8]{2,4,3,1,0:T(8,128)(2,1)} copy(bf16[8,4,128,32,8]{2,4,1,3,0:T(8,128)(2,1)S(1)} %bitcast.23) | data formatting | bytes 4194304 | tf_op jit(solution)/shard_map/transpose | solution.py:289
  14.5 0.0 copy-start.5
  14.5 0.0 copy-start.2
  14.5 2.9 %copy.15.queries_ref = bf16[8,4,128,256]{3,2,1,0:T(8,128)(2,1)S(1)} copy(bf16[8,4,128,256]{2,3,1,0:T(8,128)(2,1)} %bitcast.22) | data formatting | bytes 4194304 | tf_op jit(solution)/shard_map/reshape | solution.py:289
  17.4 0.0 copy-done.5
  17.4 0.1 broadcast_in_dim.34.length_ref
  17.5 0.0 copy-done.2
  17.5 0.0 copy-done.3
  17.5 3.4 %copy-done = bf16[8,8,16,4096]{3,2,1,0:T(8,128)(2,1)S(1)} copy-done((bf16[8,8,16,4096]{3,2,1,0:T(8,128)(2,1)S(1)}, bf16[8,8,16,4096]{3,2,1,0:T(8,128)(2,1)}, u32[]{:S(2)}) %copy-start) | copy-done | bytes 8388632
  20.9 1.0 %copy-done.1 = bf16[8,32,1024]{2,1,0:T(8,128)(2,1)S(1)} copy-done((bf16[8,32,1024]{2,1,0:T(8,128)(2,1)S(1)}, bf16[8,32,1024]{2,1,0:T(8,128)(2,1)}, u32[]{:S(2)}) %copy-start.1) | copy-done | bytes 524312
  22.0 5.3 %direct.1.direct_ref = f32[8,8,128]{2,1,0:T(8,128)S(1)} custom-call(s32[8]{0:T(128)S(1)} %copy-done.3, bf16[8,128,4096]{2,1,0:T(8,128)(2,1)S(1)} %bitcast.18, bf16[8,32,1024]{2,1,0:T(8,128)(2,1)S(1)} %copy-done.1, bf16[32,128]{1,0:T(8,128)(2,1)S(1)} %bitcast.21, s32[8,8,128]{2,1,0:T(8,128)S(1)} %broadcast_in_dim.34.length_ref), custom_call_target="tpu_custom_call" | custom-call | flops 536870912 | bytes 8388608 | tf_op jit(solution)/shard_map/direct/pallas_call | solution.py:259
  27.4 0.1 compare_select_fusion.weight_ref
  27.5 0.1 fusion.1.pick_ref
  27.6 8.0 %all-to-all-done = bf16[16,144,256]{2,1,0:T(8,128)(2,1)S(1)} async-done(((bf16[16,144,256]{2,1,0:T(8,128)(2,1)}), bf16[16,144,256]{2,1,0:T(8,128)(2,1)S(1)}, u32[]{:S(2)}, u32[]{:S(2)}) %all-to-all-start) | async-done | bytes 1179680 | tf_op jit(solution)/shard_map/all_to_all | solution.py:255
  35.6 0.1 broadcast_in_dim.35.row_ref
  35.7 2.9 %channel.1 = f32[16,128]{1,0:T(8,128)S(1)} custom-call(s32[3,64]{1,0:T(4,128)S(1)} %pad_add_fusion.at_ref, bf16[2304,256]{1,0:T(8,128)(2,1)S(1)} %bitcast.19, bf16[8,4,128,256]{3,2,1,0:T(8,128)(2,1)S(1)} %copy.15.queries_ref, f32[8,8,128]{2,1,0:T(8,128)S(1)} %direct.1.direct_ref, s32[8,8,128]{2,1,0:T(8,128)S(1)} %broadcast_in_dim.34.length_ref, ...), custom_call_target="tpu_custom_call" | custom-call | tf_op jit(solution)/shard_map/channel/pallas_call | solution.py:308
  38.6 13.7 %all_to_all.14 = f32[16,1,128]{2,1,0:T(1,128)S(1)} all-to-all(f32[16,1,128]{2,1,0:T(1,128)S(1)} %bitcast.20), channel_id=1, replica_groups=mesh['group'=2,'dp'=16] {'dp'}, dimensions={0} | all-to-all | bytes 16384 | tf_op jit(solution)/shard_map/all_to_all | solution.py:330
  52.3 0.5 %reduce_sum.9 = f32[128]{0:T(128)} reduce(f32[16,1,128]{2,1,0:T(1,128)S(1)} %all_to_all.14, f32[]{:T(128)} %constant.99.clone.1), dimensions={0,1}, to_apply=%region_0.1 | reduce | flops 1920 | bytes 8708 | tf_op jit(solution)/shard_map/reduce_sum | solution.py:331
  (12 shorter events, 0.1 us)
Async XLA Ops:
  0.0 10.5 %copy-start.4 = (s32[8,8]{1,0:T(8,128)S(1)}, s32[8,8]{1,0:T(8,128)}, u32[]{:S(2)}) copy-start(s32[8,8]{1,0:T(8,128)} %param.15) | copy-start | bytes 772
  3.1 32.5 %all-to-all-start = ((bf16[16,144,256]{2,1,0:T(8,128)(2,1)}), bf16[16,144,256]{2,1,0:T(8,128)(2,1)S(1)}, u32[]{:S(2)}, u32[]{:S(2)}) async-start(bf16[16,144,256]{2,1,0:T(8,128)(2,1)} %pack.1), calls=%async_computation | async-start | bytes 2359296 | tf_op jit(solution)/shard_map/all_to_all | solution.py:255
  14.5 2.9 %copy-start.5 = (s32[8,8]{1,0:T(8,128)S(1)}, s32[8,8]{1,0:T(8,128)}, u32[]{:S(2)}) copy-start(s32[8,8]{1,0:T(8,128)} %param.14) | copy-start | bytes 772
  14.5 3.0 %copy-start.2 = (bf16[4096]{0:T(1024)(128)(2,1)S(1)}, bf16[4096]{0:T(1024)(128)(2,1)}, u32[]{:S(2)}) copy-start(bf16[4096]{0:T(1024)(128)(2,1)} %param.16) | copy-start | bytes 24580
  14.5 3.0 %copy-start.3 = (s32[8]{0:T(128)S(1)}, s32[8]{0:T(128)}, u32[]{:S(2)}) copy-start(s32[8]{0:T(128)} %target_length.1) | copy-start | bytes 100
  17.5 3.4 %copy-start = (bf16[8,8,16,4096]{3,2,1,0:T(8,128)(2,1)S(1)}, bf16[8,8,16,4096]{3,2,1,0:T(8,128)(2,1)}, u32[]{:S(2)}) copy-start(bf16[8,8,16,4096]{3,2,1,0:T(8,128)(2,1)} %param.9) | copy-start | bytes 25165828
  20.9 1.0 %copy-start.1 = (bf16[8,32,1024]{2,1,0:T(8,128)(2,1)S(1)}, bf16[8,32,1024]{2,1,0:T(8,128)(2,1)}, u32[]{:S(2)}) copy-start(bf16[8,32,1024]{2,1,0:T(8,128)(2,1)} %states_ref.1) | copy-start | bytes 1572868

commit v3 on v2

--- a/solution.py
+++ b/solution.py
@@ -13,7 +13,6 @@
 LANES = 128
 SUBLANES = 8
 MASKED = -1e30
-PACK_LIMIT = 60 * 2**20
 
 bf16 = jnp.bfloat16
 f32 = jnp.float32
@@ -36,31 +35,25 @@
     half = width // 2
     heads = read_ref.shape[0]
     share = heads // KEY_VALUE_HEADS
-    parts = (sems.shape[0] - 1) // 4
-    step = peers // parts
-    load_readout = pltpu.make_async_copy(readout_ref, read_ref, sems.at[0])
-    load_readout.start()
-    loads, moves, sends = [], [], []
-    for i in range(parts):
-        at = pl.ds(i * step, step)
-        loads.append(
-            pltpu.make_async_copy(
-                states_ref.at[at, :, width:], values_ref.at[at], sems.at[1 + i]
-            )
+    keep = [slice(0, body), slice(body, 2 * body), slice(2 * body, None)]
+    loads = [
+        pltpu.make_async_copy(
+            states_ref.at[:, :, j * half : (j + 1) * half], sent_ref.at[:, keep[j], :], sems.at[j]
         )
-        loads[i].start()
-    for i in range(parts):
-        at = pl.ds(i * step, step)
-        for j in range(2):
-            moves.append(
-                pltpu.make_async_copy(
-                    states_ref.at[at, :, j * half : (j + 1) * half],
-                    sent_ref.at[at, j * body : (j + 1) * body, :],
-                    sems.at[1 + (1 + j) * parts + i],
-                )
-            )
-            moves[-1].start()
-    load_readout.wait()
+        for j in range(2)
+    ]
+    loads.append(pltpu.make_async_copy(states_ref.at[:, :, width:], values_ref, sems.at[2]))
+    loads.append(pltpu.make_async_copy(readout_ref, read_ref, sems.at[3]))
+    sends = [
+        pltpu.make_async_copy(sent_ref.at[:, keep[j], :], out_ref.at[:, keep[j], :], sems.at[4 + j])
+        for j in range(3)
+    ]
+    for copy in loads:
+        copy.start()
+    for j in range(2):
+        loads[j].wait()
+        sends[j].start()
+    loads[3].wait()
     repeated = jnp.concatenate([read_ref[...]] * (LANES // heads), axis=0)
     group = iota((LANES, HEAD_SIZE), 0) % heads // share
     spread = jnp.concatenate(
@@ -68,32 +61,34 @@
         axis=1,
     )
     lane = iota((keys, LANES), 1)
-    for i in range(parts):
-        loads[i].wait()
-        read = dot_nt(values_ref[i * step : (i + 1) * step].reshape(step * body, width), spread)
-        for p in range(step):
-            for j in range(half // LANES):
-                even = min(2 * j, rows - 1)
-                odd = min(2 * j + 1, rows - 1)
-                even = read[p * body + even * keys : p * body + (even + 1) * keys, :]
-                odd = read[p * body + odd * keys : p * body + (odd + 1) * keys, :]
-                value = jnp.where(lane < 2 * heads, even, odd)
-                high = value.astype(bf16).astype(f32)
-                value = jnp.where(lane % (2 * heads) < heads, high, value - high)
-                sent_ref[i * step + p, 2 * body :, j * LANES : (j + 1) * LANES] = value.astype(bf16)
-        moves[2 * i].wait()
-        moves[2 * i + 1].wait()
-        at = pl.ds(i * step, step)
-        sends.append(
-            pltpu.make_async_copy(sent_ref.at[at], out_ref.at[at], sems.at[1 + 3 * parts + i])
-        )
-        sends[i].start()
+    loads[2].wait()
+    read = dot_nt(values_ref[...].reshape(peers * body, width), spread)
+    for p in range(peers):
+        for j in range(half // LANES):
+            even = min(2 * j, rows - 1)
+            odd = min(2 * j + 1, rows - 1)
+            even = read[p * body + even * keys : p * body + (even + 1) * keys, :]
+            odd = read[p * body + odd * keys : p * body + (odd + 1) * keys, :]
+            value = jnp.where(lane < 2 * heads, even, odd)
+            high = value.astype(bf16).astype(f32)
+            value = jnp.where(lane % (2 * heads) < heads, high, value - high)
+            sent_ref[p, keep[2], j * LANES : (j + 1) * LANES] = value.astype(bf16)
+    sends[2].start()
     for copy in sends:
         copy.wait()
 
 
-def direct_kernel(target_length, queries_ref, states_ref, readout_ref, length_ref, out_ref):
+def direct_kernel(
+    target_length, at_ref, queries_ref, states_ref, readout_ref, length_ref, out_ref, place_ref
+):
     t = pl.program_id(0)
+
+    @pl.when(t == 0)
+    def _():
+        for i in range(at_ref.shape[0]):
+            for j in range(at_ref.shape[1]):
+                place_ref[i, j] = at_ref[i, j]
+
     keys = states_ref.shape[1]
     width = states_ref.shape[2] // 2
     tokens = queries_ref.shape[1]
@@ -233,7 +228,6 @@
 
     body = rows * keys
     chunk = 2 * body + keys
-    parts = 4
     hbm = pl.BlockSpec(memory_space=pltpu.HBM)
     packed = pl.pallas_call(
         functools.partial(pack_kernel, rows, keys),
@@ -244,31 +238,47 @@
             pltpu.VMEM((peers, body, width), bf16),
             pltpu.VMEM((heads, HEAD_SIZE), bf16),
             pltpu.VMEM((peers, chunk, width // 2), bf16),
-            pltpu.SemaphoreType.DMA((1 + 4 * parts,)),
+            pltpu.SemaphoreType.DMA((7,)),
         ],
-        compiler_params=pltpu.CompilerParams(vmem_limit_bytes=PACK_LIMIT),
+        compiler_params=pltpu.CompilerParams(vmem_limit_bytes=16 * 2**20),
         name="pack",
     )(
-        candidate_states.reshape(peers, body, 2 * width),
-        channel_readout.reshape(heads, HEAD_SIZE),
+        pltpu.with_memory_space_constraint(
+            candidate_states.reshape(peers, body, 2 * width), pltpu.HBM
+        ),
+        pltpu.with_memory_space_constraint(channel_readout.reshape(heads, HEAD_SIZE), pltpu.HBM),
     )
     arrived = lax.all_to_all(packed, "dp", split_axis=0, concat_axis=0, tiled=True)
 
     length_lanes = jnp.broadcast_to(candidate_length[:, :, None], (targets, slots, LANES))
     row_lanes = jnp.broadcast_to(candidate_row[:, :, None], (targets, slots, LANES))
-    direct = pl.pallas_call(
+    flat = candidate_row.reshape(candidates)
+    at = jnp.stack(
+        [
+            flat // rows * chunk + flat % rows * keys,
+            flat // rows * chunk + 2 * body,
+            flat % rows // 2 * LANES,
+        ]
+    )
+    direct, place = pl.pallas_call(
         direct_kernel,
-        out_shape=jax.ShapeDtypeStruct((targets, slots, slots * keys), f32),
+        out_shape=(
+            jax.ShapeDtypeStruct((targets, slots, slots * keys), f32),
+            pltpu.SMEM(at.shape, jnp.int32),
+        ),
         grid_spec=pltpu.PrefetchScalarGridSpec(
-            num_scalar_prefetch=1,
+            num_scalar_prefetch=2,
             grid=(targets,),
             in_specs=[
-                pl.BlockSpec((1, slots * keys, query_width), lambda t, n: (t, 0, 0)),
-                pl.BlockSpec((1, tokens, 2 * width), lambda t, n: (t, 0, 0)),
-                pl.BlockSpec((heads, HEAD_SIZE), lambda t, n: (0, 0)),
-                pl.BlockSpec((1, slots, LANES), lambda t, n: (t, 0, 0)),
+                pl.BlockSpec((1, slots * keys, query_width), lambda t, n, a: (t, 0, 0)),
+                pl.BlockSpec((1, tokens, 2 * width), lambda t, n, a: (t, 0, 0)),
+                pl.BlockSpec((heads, HEAD_SIZE), lambda t, n, a: (0, 0)),
+                pl.BlockSpec((1, slots, LANES), lambda t, n, a: (t, 0, 0)),
             ],
-            out_specs=pl.BlockSpec((1, slots, slots * keys), lambda t, n: (t, 0, 0)),
+            out_specs=(
+                pl.BlockSpec((1, slots, slots * keys), lambda t, n, a: (t, 0, 0)),
+                pl.BlockSpec(memory_space=pltpu.SMEM),
+            ),
         ),
         compiler_params=pltpu.CompilerParams(vmem_limit_bytes=32 * 2**20),
         cost_estimate=pl.CostEstimate(
@@ -279,6 +289,7 @@
         name="direct",
     )(
         target_length,
+        at,
         candidate_queries.reshape(targets, slots * keys, query_width),
         target_states,
         direct_readout.reshape(heads, HEAD_SIZE),
@@ -288,14 +299,6 @@
     queries = target_queries.reshape(targets, tokens, KEY_VALUE_HEADS, share, HEAD_SIZE)
     queries = queries.transpose(0, 2, 4, 1, 3).reshape(
         targets, KEY_VALUE_HEADS, HEAD_SIZE, columns
-    )
-    flat = candidate_row.reshape(candidates)
-    at = jnp.stack(
-        [
-            flat // rows * chunk + flat % rows * keys,
-            flat // rows * chunk + 2 * body,
-            flat % rows // 2 * LANES,
-        ]
     )
     lanes = jnp.arange(LANES, dtype=jnp.int32)
     pick = lanes % share + row_lanes % rows % 2 * (2 * heads)
@@ -317,7 +320,7 @@
         compiler_params=pltpu.CompilerParams(vmem_limit_bytes=32 * 2**20),
         name="channel",
     )(
-        at,
+        place,
         arrived.reshape(peers * chunk, width // 2),
         queries,
         direct,

time: 53.2 us -> 52.5 us (0.987)
  local copies, waits for them, and re-layouts: 11.5 us -> 9.91 us
  waiting for transfers between devices: 7.98 us -> 9.33 us
    unnamed x13 -> x15, local copies, waits for them, and re-layouts: 6.51 us -> 4.92 us
    all_to_all x1, waiting for transfers between devices: 7.98 us -> 9.33 us  [on_device(): lax.all_to_all(packed, 'dp', split_axis=0, concat_axis=0, tiled=True)]
    pallas_call x1, Pallas kernels: 2.89 us -> 2.31 us  [on_device(): pl.pallas_call(functools.partial(channel_kernel, rows, share), out_shape=...]
  transfers between devices with their start and end apart: 1 -> 1, of which waited for: 1 -> 1; matrix products, arithmetic and copies ran while one was open for 14% -> 11% of each run, Pallas kernels for 10% -> 11%
where the time goes in v3:
time: 52.5 us; the launch traced here: 52.1 us
  blocking collectives  13.7 us (26%)
  Pallas kernels  10.8 us (21%)
  local copies, waits for them, and re-layouts  9.91 us (19%)
  waiting for transfers between devices  9.33 us (18%)
  starting transfers between devices  7.41 us (14%)
  other arithmetic  0.79 us (2%)
    all_to_all x1, blocking collectives, on_device(): lax.all_to_all(outgoing, 'dp', split_axis=0, concat_axis=0, tiled=True)  13.7 us
    all_to_all x1, waiting for transfers between devices, on_device(): lax.all_to_all(packed, 'dp', split_axis=0, concat_axis=0, tiled=True)  9.33 us
    all_to_all x1, starting transfers between devices, on_device(): lax.all_to_all(packed, 'dp', split_axis=0, concat_axis=0, tiled=True)  7.41 us
    pallas_call x1, Pallas kernels, on_device(): pl.pallas_call(direct_kernel, out_shape=(jax.ShapeDtypeStruct((targets, s...  5.6 us
    unnamed x15, local copies, waits for them, and re-layouts  4.92 us
    pallas_call x1, Pallas kernels, on_device(): pl.pallas_call(functools.partial(pack_kernel, rows, keys), out_shape=jax....  2.89 us
    reshape x1, local copies, waits for them, and re-layouts, on_device(): queries.transpose(0, 2, 4, 1, 3)  2.89 us
    pallas_call x1, Pallas kernels, on_device(): pl.pallas_call(functools.partial(channel_kernel, rows, share), out_shape=...  2.31 us
  transfers between devices with their start and end apart: 1, of which 1 were waited for; matrix products, arithmetic and copies ran while one was open for 11% of the time, Pallas kernels for 11%

profile of v3, /device:TPU:0, one launch (start us, length us, event | category | flops | bytes accessed | tf_op | source)
XLA Modules:
  0.0 52.1 jit_solution(18068602058791012809)
XLA Ops:
  0.0 0.0 copy-start.5
  0.0 0.0 copy-start.4
  0.0 2.9 %pack.1 = bf16[16,144,256]{2,1,0:T(8,128)(2,1)} custom-call(bf16[16,64,1024]{2,1,0:T(8,128)(2,1)} %bitcast.24, bf16[32,128]{1,0:T(8,128)(2,1)} %bitcast.26), custom_call_target="tpu_custom_call" | custom-call | tf_op jit(solution)/shard_map/pack/pallas_call | solution.py:232
  2.9 7.4 %all-to-all-start = ((bf16[16,144,256]{2,1,0:T(8,128)(2,1)}), bf16[16,144,256]{2,1,0:T(8,128)(2,1)S(1)}, u32[]{:S(2)}, u32[]{:S(2)}) async-start(bf16[16,144,256]{2,1,0:T(8,128)(2,1)} %pack.1), calls=%async_computation | async-start | bytes 2359296 | tf_op jit(solution)/shard_map/all_to_all | solution.py:251
  10.3 0.0 copy-done.5
  10.3 0.1 reshape.263
  10.4 0.0 copy-done.4
  10.4 0.5 copy.17
  10.9 1.9 %copy.19 = bf16[8,4,128,32,8]{2,4,3,1,0:T(8,128)(2,1)} copy(bf16[8,4,128,32,8]{2,4,1,3,0:T(8,128)(2,1)S(1)} %bitcast.23) | data formatting | bytes 4194304 | tf_op jit(solution)/shard_map/transpose | solution.py:300
  12.8 2.9 %copy.15.queries_ref = bf16[8,4,128,256]{3,2,1,0:T(8,128)(2,1)S(1)} copy(bf16[8,4,128,256]{2,3,1,0:T(8,128)(2,1)} %bitcast.22) | data formatting | bytes 4194304 | tf_op jit(solution)/shard_map/reshape | solution.py:300
  15.7 0.0 copy-done.6
  15.8 0.1 broadcast_in_dim.34.length_ref
  15.8 0.0 copy-done.2
  15.8 0.0 copy-done.3
  15.8 3.4 %copy-done = bf16[8,8,16,4096]{3,2,1,0:T(8,128)(2,1)S(1)} copy-done((bf16[8,8,16,4096]{3,2,1,0:T(8,128)(2,1)S(1)}, bf16[8,8,16,4096]{3,2,1,0:T(8,128)(2,1)}, u32[]{:S(2)}) %copy-start) | copy-done | bytes 8388632
  19.2 1.0 %copy-done.1 = bf16[8,32,1024]{2,1,0:T(8,128)(2,1)S(1)} copy-done((bf16[8,32,1024]{2,1,0:T(8,128)(2,1)S(1)}, bf16[8,32,1024]{2,1,0:T(8,128)(2,1)}, u32[]{:S(2)}) %copy-start.1) | copy-done | bytes 524312
  20.3 5.6 %direct.1 = (f32[8,8,128]{2,1,0:T(8,128)S(1)}, s32[3,64]{1,0:T(4,128)S(4)}) custom-call(s32[8]{0:T(128)S(1)} %copy-done.3, s32[3,64]{1,0:T(4,128)S(1)} %pad_add_fusion.at_ref, bf16[8,128,4096]{2,1,0:T(8,128)(2,1)S(1)} %bitcast.18, bf16[8,32,1024]{2,1,0:T(8,128)(2,1)S(1)} %copy-done.1, bf16[32,128]{1,0:T(8,128)(2,1)S(1)} %bitcast.21, ...), custom_call_target="tpu_custom_call" | custom-call | flops 536870912 | bytes 8388608 | tf_op jit(solution)/shard_map/direct/pallas_call | solution.py:263
  25.9 0.1 compare_select_fusion.weight_ref
  26.0 0.1 fusion.1.pick_ref
  26.1 9.3 %all-to-all-done = bf16[16,144,256]{2,1,0:T(8,128)(2,1)S(1)} async-done(((bf16[16,144,256]{2,1,0:T(8,128)(2,1)}), bf16[16,144,256]{2,1,0:T(8,128)(2,1)S(1)}, u32[]{:S(2)}, u32[]{:S(2)}) %all-to-all-start) | async-done | bytes 1179680 | tf_op jit(solution)/shard_map/all_to_all | solution.py:251
  35.5 0.1 broadcast_in_dim.35.row_ref
  35.5 2.3 %channel.1 = f32[16,128]{1,0:T(8,128)S(1)} custom-call(s32[3,64]{1,0:T(4,128)S(4)} %get-tuple-element.7.at_ref, bf16[2304,256]{1,0:T(8,128)(2,1)S(1)} %bitcast.19, bf16[8,4,128,256]{3,2,1,0:T(8,128)(2,1)S(1)} %copy.15.queries_ref, f32[8,8,128]{2,1,0:T(8,128)S(1)} %get-tuple-element.8.direct_ref, s32[8,8,128]{2,1,0:T(8,128)S(1)} %broadcast_in_dim.34.length_ref, ...), custom_call_target="tpu_custom_call" | custom-call | tf_op jit(solution)/shard_map/channel/pallas_call | solution.py:311
  37.8 13.7 %all_to_all.14 = f32[16,1,128]{2,1,0:T(1,128)S(1)} all-to-all(f32[16,1,128]{2,1,0:T(1,128)S(1)} %bitcast.20), channel_id=1, replica_groups=mesh['group'=2,'dp'=16] {'dp'}, dimensions={0} | all-to-all | bytes 16384 | tf_op jit(solution)/shard_map/all_to_all | solution.py:333
  51.5 0.5 %reduce_sum.9 = f32[128]{0:T(128)} reduce(f32[16,1,128]{2,1,0:T(1,128)S(1)} %all_to_all.14, f32[]{:T(128)} %constant.99.clone.1), dimensions={0,1}, to_apply=%region_0.1 | reduce | flops 1920 | bytes 8708 | tf_op jit(solution)/shard_map/reduce_sum | solution.py:334
  (14 shorter events, 0.1 us)
Async XLA Ops:
  0.0 10.3 %copy-start.5 = (s32[8,8]{1,0:T(8,128)S(1)}, s32[8,8]{1,0:T(8,128)}, u32[]{:S(2)}) copy-start(s32[8,8]{1,0:T(8,128)} %param.15) | copy-start | bytes 772
  0.0 10.4 %copy-start.4 = (bf16[8,32,4096]{2,1,0:T(8,128)(2,1)S(1)}, bf16[8,32,4096]{2,1,0:T(8,128)(2,1)}, u32[]{:S(2)}) copy-start(bf16[8,32,4096]{2,1,0:T(8,128)(2,1)} %param.11) | copy-start | bytes 6291460
  2.9 32.5 %all-to-all-start = ((bf16[16,144,256]{2,1,0:T(8,128)(2,1)}), bf16[16,144,256]{2,1,0:T(8,128)(2,1)S(1)}, u32[]{:S(2)}, u32[]{:S(2)}) async-start(bf16[16,144,256]{2,1,0:T(8,128)(2,1)} %pack.1), calls=%async_computation | async-start | bytes 2359296 | tf_op jit(solution)/shard_map/all_to_all | solution.py:251
  12.8 3.0 %copy-start.6 = (s32[8,8]{1,0:T(8,128)S(1)}, s32[8,8]{1,0:T(8,128)}, u32[]{:S(2)}) copy-start(s32[8,8]{1,0:T(8,128)} %param.14) | copy-start | bytes 772
  12.8 3.0 %copy-start.2 = (bf16[4096]{0:T(1024)(128)(2,1)S(1)}, bf16[4096]{0:T(1024)(128)(2,1)}, u32[]{:S(2)}) copy-start(bf16[4096]{0:T(1024)(128)(2,1)} %param.16) | copy-start | bytes 24580
  12.8 3.0 %copy-start.3 = (s32[8]{0:T(128)S(1)}, s32[8]{0:T(128)}, u32[]{:S(2)}) copy-start(s32[8]{0:T(128)} %target_length.1) | copy-start | bytes 100
  15.8 3.4 %copy-start = (bf16[8,8,16,4096]{3,2,1,0:T(8,128)(2,1)S(1)}, bf16[8,8,16,4096]{3,2,1,0:T(8,128)(2,1)}, u32[]{:S(2)}) copy-start(bf16[8,8,16,4096]{3,2,1,0:T(8,128)(2,1)} %param.9) | copy-start | bytes 25165828
  19.2 1.0 %copy-start.1 = (bf16[8,32,1024]{2,1,0:T(8,128)(2,1)S(1)}, bf16[8,32,1024]{2,1,0:T(8,128)(2,1)}, u32[]{:S(2)}) copy-start(bf16[8,32,1024]{2,1,0:T(8,128)(2,1)} %states_ref.1) | copy-start | bytes 1572868

commit v4 on v3

v4 whole, which is shorter than its diff:
```python
import functools
import math

import jax
import jax.numpy as jnp
from jax import lax
from jax.experimental import pallas as pl
from jax.experimental.pallas import tpu as pltpu
from jax.sharding import PartitionSpec as P

KEY_VALUE_HEADS = 4
HEAD_SIZE = 128
LANES = 128
SUBLANES = 8
MASKED = -1e30
PACKED = 4
KEY_PARTS = 2

bf16 = jnp.bfloat16
f32 = jnp.float32


def dot_nt(a, b):
    return lax.dot_general(a, b, (((1,), (1,)), ((), ())), preferred_element_type=f32)


def dot_nn(a, b):
    return lax.dot_general(a, b, (((1,), (0,)), ((), ())), preferred_element_type=f32)


def iota(shape, axis):
    return lax.broadcasted_iota(jnp.int32, shape, axis)


def keys_kernel(states_ref, out_ref, held_ref, sems):
    peers, _, width = out_ref.shape
    parts = sems.shape[1]
    step = peers // parts
    loads, sends = [], []
    for i in range(parts):
        at = pl.ds(i * step, step)
        loads.append(
            pltpu.make_async_copy(states_ref.at[at, :, :width], held_ref.at[at], sems.at[0, i])
        )
        sends.append(pltpu.make_async_copy(held_ref.at[at], out_ref.at[at], sems.at[1, i]))
        loads[i].start()
    for i in range(parts):
        loads[i].wait()
        sends[i].start()
    for copy in sends:
        copy.wait()


def value_kernel(rows, keys, values_ref, readout_ref, factor_ref, first_ref, read_ref):
    peers, body, width = values_ref.shape
    share = readout_ref.shape[0] // KEY_VALUE_HEADS
    wide = LANES // KEY_VALUE_HEADS
    blocks = []
    for g in range(KEY_VALUE_HEADS):
        block = jnp.concatenate(
            [readout_ref[g * share : (g + 1) * share, :].astype(f32)] * (wide // share), axis=0
        )
        none = jnp.zeros_like(block)
        blocks.append(
            jnp.concatenate([block if i == g else none for i in range(KEY_VALUE_HEADS)], axis=1)
        )
    spread = jnp.concatenate(blocks, axis=0).astype(bf16)
    read_ref[...] = dot_nt(values_ref[...].reshape(peers * body, width), spread)
    part = iota((PACKED, LANES), 1) % wide // share
    first_key = (iota((PACKED, LANES), 0) == 0) & (part == 0)
    if rows < PACKED:
        factor_ref[...] = jnp.zeros_like(factor_ref)
    first_ref[...] = jnp.zeros_like(first_ref)
    for p in range(peers):
        for r in range(rows):
            start = p * body + r * keys
            value = read_ref[pl.ds(start, PACKED, stride=PACKED), :]
            for i in range(1, PACKED):
                value = jnp.where(part == i, read_ref[pl.ds(start + i, PACKED, stride=PACKED), :], value)
            first = read_ref[start : start + 1, :]
            factor_ref[p, pl.ds(r, PACKED, stride=PACKED), :] = jnp.where(first_key, 1.0, value - first)
            first_ref[p, r : r + 1, :] = jnp.where(part[:1] == 0, first, 0.0)


def direct_kernel(
    target_length, at_ref, queries_ref, states_ref, readout_ref, length_ref, out_ref, place_ref
):
    t = pl.program_id(0)

    @pl.when(t == 0)
    def _():
        for i in range(at_ref.shape[0]):
            for j in range(at_ref.shape[1]):
                place_ref[i, j] = at_ref[i, j]

    keys = states_ref.shape[1]
    width = states_ref.shape[2] // 2
    tokens = queries_ref.shape[1]
    slots = length_ref.shape[1]
    heads = readout_ref.shape[0]
    share = heads // KEY_VALUE_HEADS
    scale = math.log2(math.e) / math.sqrt(HEAD_SIZE)
    usable = iota((keys, share * tokens), 0) < target_length[t]
    total = jnp.zeros((1, tokens), f32)
    for g in range(KEY_VALUE_HEADS):
        k = states_ref[0, :, g * HEAD_SIZE : (g + 1) * HEAD_SIZE]
        v = states_ref[0, :, width + g * HEAD_SIZE : width + (g + 1) * HEAD_SIZE]
        q = jnp.concatenate(
            [
                queries_ref[0, :, h * HEAD_SIZE : (h + 1) * HEAD_SIZE]
                for h in range(g * share, (g + 1) * share)
            ],
            axis=0,
        )
        scores = jnp.where(usable, dot_nt(k, q), MASKED)
        weights = jnp.exp2((scores - jnp.max(scores, axis=0, keepdims=True)) * scale)
        read = dot_nt(v, readout_ref[g * share : (g + 1) * share, :])
        read = jnp.concatenate(
            [jnp.broadcast_to(read[:, h : h + 1], (keys, tokens)) for h in range(share)], axis=1
        )
        ratio = jnp.sum(weights * read, axis=0, keepdims=True) / jnp.sum(
            weights, axis=0, keepdims=True
        )
        for h in range(share):
            total = total + ratio[:, h * tokens : (h + 1) * tokens]
    source = tokens // slots
    lane = iota((slots, tokens), 1)
    length = length_ref[0]
    wanted = (lane // source == iota((slots, tokens), 0)) & (lane % source < length)
    total = jnp.where(wanted, jnp.broadcast_to(total, (slots, tokens)), 0.0)
    total = jnp.sum(total, axis=1, keepdims=True) / length.astype(f32)
    out_ref[0] = jnp.where(lane == 0, total, 0.0)


def halves(a, b, bit, lane):
    upper = lane // bit % 2 == 1
    moved = jnp.where(upper, a, b)
    if 2 * bit == LANES:
        moved = pltpu.roll(moved, bit, 1)
    else:
        moved = jnp.take_along_axis(moved, lane + jnp.where(upper, -bit, bit), axis=1)
    return jnp.where(upper, b, a) + moved


def channel_kernel(
    rows,
    place_ref,
    arrived_ref,
    queries_ref,
    direct_ref,
    length_ref,
    weight_ref,
    out_ref,
    keys_ref,
    pooled_ref,
):
    targets = queries_ref.shape[0]
    columns = queries_ref.shape[3]
    slots = direct_ref.shape[1]
    peers = out_ref.shape[0]
    keys = keys_ref.shape[2] // slots
    wide = LANES // KEY_VALUE_HEADS
    share = wide // PACKED
    scale = math.log2(math.e) / math.sqrt(HEAD_SIZE)
    position = iota((keys, slots, columns), 0)
    lane = iota((slots, LANES), 1)
    for t in range(targets):
        for s in range(slots):
            start = pl.multiple_of(place_ref[0, t * slots + s], keys)
            key = arrived_ref[pl.ds(start, keys), :].astype(f32)
            for g in range(KEY_VALUE_HEADS):
                keys_ref[t, g, pl.ds(s, keys, stride=slots), :] = key[
                    :, g * HEAD_SIZE : (g + 1) * HEAD_SIZE
                ]
        usable = position < jnp.concatenate([length_ref[t]] * (columns // LANES), axis=1)[None]
        parts = []
        for g in range(KEY_VALUE_HEADS):
            scores = dot_nn(keys_ref[t, g].astype(bf16), queries_ref[t, g])
            scores = jnp.where(usable, scores.reshape(keys, slots, columns), MASKED)
            weights = jnp.exp2((scores - jnp.max(scores, axis=0, keepdims=True)) * scale)
            weights = weights * (weight_ref[t : t + 1, :] / jnp.sum(weights, axis=0))[None]
            part = weights[:, :, :LANES]
            for i in range(1, columns // LANES):
                part = part + weights[:, :, i * LANES : (i + 1) * LANES]
            parts.append(part)
        for i in range(keys // PACKED):
            part = []
            for k in range(i * PACKED, (i + 1) * PACKED):
                low = halves(parts[0][k], parts[2][k], 2 * wide, lane)
                high = halves(parts[1][k], parts[3][k], 2 * wide, lane)
                part.append(halves(low, high, wide, lane))
            low = halves(part[0], part[2], 2 * share, lane)
            high = halves(part[1], part[3], 2 * share, lane)
            part = halves(low, high, share, lane)
            if i == 0:
                part = jnp.where(lane % wide < share, direct_ref[t], part)
            start = (t * (keys // PACKED) + i) * slots
            pooled_ref[start : start + slots, :] = part
    if rows < PACKED:
        out_ref[...] = jnp.zeros_like(out_ref)
    for p in range(peers):
        for r in range(rows):
            out_ref[p, pl.ds(r, PACKED, stride=PACKED), :] = pooled_ref[
                pl.ds(place_ref[1, p * rows + r], PACKED, stride=slots), :
            ]


def finish_kernel(rows, returned_ref, factor_ref, first_ref, out_ref):
    total = returned_ref[...] * factor_ref[...]
    total = total[:, :SUBLANES] + total[:, SUBLANES:] + first_ref[...]
    total = jnp.sum(total, axis=2, keepdims=True)
    shape = (total.shape[0], SUBLANES, LANES)
    at = iota(shape, 0) * rows + iota(shape, 1) % PACKED
    total = jnp.where((iota(shape, 2) == at) & (iota(shape, 1) % PACKED < rows), total, 0.0)
    total = jnp.sum(jnp.sum(total, axis=0), axis=0, keepdims=True)
    out_ref[...] = total[:, : out_ref.shape[1]]


def on_device(
    candidate_queries,
    target_states,
    target_queries,
    candidate_states,
    target_length,
    candidate_length,
    candidate_row,
    direct_readout,
    channel_readout,
    *,
    peers,
):
    targets, slots, keys, query_width = candidate_queries.shape
    tokens = target_queries.shape[1]
    candidates = candidate_states.shape[0]
    width = candidate_states.shape[2] // 2
    heads = query_width // HEAD_SIZE
    share = heads // KEY_VALUE_HEADS
    rows = candidates // peers
    columns = share * tokens
    assert slots == SUBLANES and keys == 2 * SUBLANES and slots * keys == LANES
    assert 4 * heads == LANES and width == 4 * LANES and rows <= 4 and candidates <= LANES

    body = rows * keys
    vmem = pl.BlockSpec(memory_space=pltpu.VMEM)
    smem = pl.BlockSpec(memory_space=pltpu.SMEM)
    assert keys == PACKED * PACKED and rows <= PACKED and share == LANES // KEY_VALUE_HEADS // PACKED
    hbm = pl.BlockSpec(memory_space=pltpu.HBM)
    sent = pl.pallas_call(
        keys_kernel,
        out_shape=jax.ShapeDtypeStruct((peers, body, width), bf16),
        in_specs=[hbm],
        out_specs=hbm,
        scratch_shapes=[
            pltpu.VMEM((peers, body, width), bf16),
            pltpu.SemaphoreType.DMA((2, KEY_PARTS)),
        ],
        compiler_params=pltpu.CompilerParams(vmem_limit_bytes=16 * 2**20),
        name="keys",
    )(pltpu.with_memory_space_constraint(candidate_states.reshape(peers, body, 2 * width), pltpu.HBM))
    arrived = lax.all_to_all(sent, "dp", split_axis=0, concat_axis=0, tiled=True)

    step = max(1, peers // 4)
    factor, first = pl.pallas_call(
        functools.partial(value_kernel, rows, keys),
        out_shape=(
            jax.ShapeDtypeStruct((peers, keys, LANES), f32),
            jax.ShapeDtypeStruct((peers, SUBLANES, LANES), f32),
        ),
        grid=(peers // step,),
        in_specs=[
            pl.BlockSpec((step, body, width), lambda i: (i, 0, 1)),
            pl.BlockSpec((heads, HEAD_SIZE), lambda i: (0, 0)),
        ],
        out_specs=(
            pl.BlockSpec((step, keys, LANES), lambda i: (i, 0, 0)),
            pl.BlockSpec((step, SUBLANES, LANES), lambda i: (i, 0, 0)),
        ),
        scratch_shapes=[pltpu.VMEM((step * body, LANES), f32)],
        compiler_params=pltpu.CompilerParams(vmem_limit_bytes=16 * 2**20),
        cost_estimate=pl.CostEstimate(
            flops=2 * LANES * width * candidates * keys,
            bytes_accessed=candidate_states.size,
            transcendentals=0,
        ),
        name="value",
    )(
        candidate_states.reshape(peers, body, 2 * width),
        channel_readout.reshape(heads, HEAD_SIZE),
    )

    length_lanes = jnp.broadcast_to(candidate_length[:, :, None], (targets, slots, LANES))
    flat = candidate_row.reshape(candidates)
    pair = jnp.arange(candidates, dtype=jnp.int32)
    start = pair // slots * (slots * PACKED) + pair % slots
    start = jnp.sum(jnp.where(flat[None, :] == pair[:, None], start[None, :], 0), axis=1)
    at = jnp.stack([flat * keys, start])
    direct, place = pl.pallas_call(
        direct_kernel,
        out_shape=(
            jax.ShapeDtypeStruct((targets, slots, slots * keys), f32),
            pltpu.SMEM(at.shape, jnp.int32),
        ),
        grid_spec=pltpu.PrefetchScalarGridSpec(
            num_scalar_prefetch=2,
            grid=(targets,),
            in_specs=[
                pl.BlockSpec((1, slots * keys, query_width), lambda t, n, a: (t, 0, 0)),
                pl.BlockSpec((1, tokens, 2 * width), lambda t, n, a: (t, 0, 0)),
                pl.BlockSpec((heads, HEAD_SIZE), lambda t, n, a: (0, 0)),
                pl.BlockSpec((1, slots, LANES), lambda t, n, a: (t, 0, 0)),
            ],
            out_specs=(
                pl.BlockSpec((1, slots, slots * keys), lambda t, n, a: (t, 0, 0)),
                pl.BlockSpec(memory_space=pltpu.SMEM),
            ),
        ),
        compiler_params=pltpu.CompilerParams(vmem_limit_bytes=32 * 2**20),
        cost_estimate=pl.CostEstimate(
            flops=4 * candidate_queries.size * tokens,
            bytes_accessed=2 * candidate_queries.size,
            transcendentals=0,
        ),
        name="direct",
    )(
        target_length,
        at,
        candidate_queries.reshape(targets, slots * keys, query_width),
        target_states,
        direct_readout.reshape(heads, HEAD_SIZE),
        length_lanes,
    )

    queries = target_queries.reshape(targets, tokens, KEY_VALUE_HEADS, share, HEAD_SIZE)
    queries = queries.transpose(0, 2, 4, 1, 3).reshape(
        targets, KEY_VALUE_HEADS, HEAD_SIZE, columns
    )
    token = jnp.arange(columns, dtype=jnp.int32)[None, :] // share
    count = target_length[:, None]
    weight = jnp.where(token < count, 1.0 / count.astype(f32), 0.0)
    outgoing = pl.pallas_call(
        functools.partial(channel_kernel, rows),
        out_shape=jax.ShapeDtypeStruct((peers, keys, LANES), f32),
        in_specs=[smem] + [vmem] * 5,
        out_specs=vmem,
        scratch_shapes=[
            pltpu.VMEM((targets, KEY_VALUE_HEADS, slots * keys, HEAD_SIZE), f32),
            pltpu.VMEM((targets * slots * PACKED, LANES), f32),
        ],
        compiler_params=pltpu.CompilerParams(vmem_limit_bytes=32 * 2**20),
        name="channel",
    )(
        place,
        arrived.reshape(peers * body, width),
        queries,
        direct,
        length_lanes,
        weight,
    )
    returned = lax.all_to_all(outgoing, "dp", split_axis=0, concat_axis=0, tiled=True)
    result = pl.pallas_call(
        functools.partial(finish_kernel, rows),
        out_shape=jax.ShapeDtypeStruct((1, candidates), f32),
        in_specs=[vmem] * 3,
        out_specs=vmem,
        compiler_params=pltpu.CompilerParams(vmem_limit_bytes=16 * 2**20),
        name="finish",
    )(returned, factor, first)
    return result.reshape(candidates)


def solution(mesh):
    in_specs = (
        P(("group", "dp"), None, None, None),
        P(("group", "dp"), None, None),
        P(("group", "dp"), None, None),
        P(("group", "dp"), None, None),
        P(("group", "dp")),
        P(("group", "dp"), None),
        P(("group", "dp"), None),
        P(),
        P(),
    )
    out_specs = P(("group", "dp"))
    return jax.shard_map(
        functools.partial(on_device, peers=mesh.shape["dp"]),
        mesh=mesh,
        in_specs=in_specs,
        out_specs=out_specs,
        check_vma=False,
    )
```

time: 52.5 us -> 51.5 us (0.981)
  blocking collectives: 13.7 us -> 0 us
  starting transfers between devices: 7.41 us -> 14.3 us
  waiting for transfers between devices: 9.33 us -> 12 us
  Pallas kernels: 10.8 us -> 12.9 us
  local copies, waits for them, and re-layouts: 9.91 us -> 11.5 us
  other arithmetic: 0.79 us -> 0.21 us
    all_to_all x1 -> x0, blocking collectives: 13.7 us -> none  [on_device(): lax.all_to_all(outgoing, 'dp', split_axis=0, concat_axis=0, tiled=True)]
    all_to_all x1 -> x2, starting transfers between devices: 7.41 us -> 14.3 us  [the longest x1 7.4 us: on_device(): lax.all_to_all(sent, 'dp', split_axis=0, concat_axis=0, tiled=True)]
    all_to_all x1 -> x2, waiting for transfers between devices: 9.33 us -> 12 us  [the longest x1 6.75 us: on_device(): lax.all_to_all(sent, 'dp', split_axis=0, concat_axis=0, tiled=True)]
    pallas_call x2 -> x4, Pallas kernels: 5.21 us -> 6.89 us  [the longest x1 3.01 us: on_device(): pl.pallas_call(functools.partial(channel_kernel, rows), out_shape=jax.Sha...]
    unnamed x15 -> x19, local copies, waits for them, and re-layouts: 4.92 us -> 6.52 us
  transfers between devices with their start and end apart: 1 -> 2, of which waited for: 1 -> 2; matrix products, arithmetic and copies ran while one was open for 11% -> 11% of each run, Pallas kernels for 11% -> 14%
where the time goes in v4:
time: 51.5 us; the launch traced here: 51 us
  starting transfers between devices  14.3 us (28%)
  Pallas kernels  12.9 us (25%)
  waiting for transfers between devices  12 us (23%)
  local copies, waits for them, and re-layouts  11.5 us (22%)
    all_to_all x1, starting transfers between devices, on_device(): lax.all_to_all(sent, 'dp', split_axis=0, concat_axis=0, tiled=True)  7.4 us
    all_to_all x1, starting transfers between devices, on_device(): lax.all_to_all(outgoing, 'dp', split_axis=0, concat_axis=0, tiled=True)  6.86 us
    all_to_all x1, waiting for transfers between devices, on_device(): lax.all_to_all(sent, 'dp', split_axis=0, concat_axis=0, tiled=True)  6.75 us
    unnamed x19, local copies, waits for them, and re-layouts  6.52 us
    pallas_call x1, Pallas kernels, on_device(): pl.pallas_call(direct_kernel, out_shape=(jax.ShapeDtypeStruct((targets, s...  6 us
    all_to_all x1, waiting for transfers between devices, on_device(): lax.all_to_all(outgoing, 'dp', split_axis=0, concat_axis=0, tiled=True)  5.25 us
    pallas_call x1, Pallas kernels, on_device(): pl.pallas_call(functools.partial(channel_kernel, rows), out_shape=jax.Sha...  3.01 us
    reshape x1, local copies, waits for them, and re-layouts, on_device(): queries.transpose(0, 2, 4, 1, 3)  2.89 us
  transfers between devices with their start and end apart: 2, of which 2 were waited for; matrix products, arithmetic and copies ran while one was open for 11% of the time, Pallas kernels for 14%

profile of v4, /device:TPU:0, one launch (start us, length us, event | category | flops | bytes accessed | tf_op | source)
XLA Modules:
  0.0 51.0 jit_solution(1583008526733783435)
XLA Ops:
  0.0 2.2 %keys.1 = bf16[16,64,512]{2,1,0:T(8,128)(2,1)} custom-call(bf16[16,64,1024]{2,1,0:T(8,128)(2,1)} %bitcast.17), custom_call_target="tpu_custom_call" | custom-call | tf_op jit(solution)/shard_map/keys/pallas_call | solution.py:248
  2.2 7.4 %all-to-all-start = ((bf16[16,64,512]{2,1,0:T(8,128)(2,1)}), bf16[16,64,512]{2,1,0:T(8,128)(2,1)S(1)}, u32[]{:S(2)}, u32[]{:S(2)}) async-start(bf16[16,64,512]{2,1,0:T(8,128)(2,1)} %keys.1), calls=%async_computation | async-start | bytes 2097152 | tf_op jit(solution)/shard_map/all_to_all | solution.py:260
  9.6 0.0 copy-done.7
  9.6 0.1 eq.17
  9.7 0.1 mul.28
  9.8 0.0 copy-done.6
  9.8 0.5 copy.16
  10.3 1.9 %copy.18 = bf16[8,4,128,32,8]{2,4,3,1,0:T(8,128)(2,1)} copy(bf16[8,4,128,32,8]{2,4,1,3,0:T(8,128)(2,1)S(1)} %bitcast.23) | data formatting | bytes 4194304 | tf_op jit(solution)/shard_map/transpose | solution.py:334
  12.2 2.9 %copy.15.queries_ref = bf16[8,4,128,256]{3,2,1,0:T(8,128)(2,1)S(1)} copy(bf16[8,4,128,256]{2,3,1,0:T(8,128)(2,1)} %bitcast.22) | data formatting | bytes 4194304 | tf_op jit(solution)/shard_map/reshape | solution.py:334
  15.1 0.1 select_reduce_fusion
  15.2 0.0 copy-done.8
  15.2 0.1 broadcast_in_dim.36.length_ref
  15.3 3.4 %copy-done = bf16[8,8,16,4096]{3,2,1,0:T(8,128)(2,1)S(1)} copy-done((bf16[8,8,16,4096]{3,2,1,0:T(8,128)(2,1)S(1)}, bf16[8,8,16,4096]{3,2,1,0:T(8,128)(2,1)}, u32[]{:S(2)}) %copy-start) | copy-done | bytes 8388632
  18.7 1.0 %copy-done.2 = bf16[8,32,1024]{2,1,0:T(8,128)(2,1)S(1)} copy-done((bf16[8,32,1024]{2,1,0:T(8,128)(2,1)S(1)}, bf16[8,32,1024]{2,1,0:T(8,128)(2,1)}, u32[]{:S(2)}) %copy-start.2) | copy-done | bytes 524312
  19.7 6.0 %direct.1 = (f32[8,8,128]{2,1,0:T(8,128)S(1)}, s32[2,64]{1,0:T(2,128)S(4)}) custom-call(s32[8]{0:T(128)S(1)} %copy-done.5, s32[2,64]{1,0:T(2,128)S(1)} %pad_add_fusion.at_ref, bf16[8,128,4096]{2,1,0:T(8,128)(2,1)S(1)} %bitcast.16, bf16[8,32,1024]{2,1,0:T(8,128)(2,1)S(1)} %copy-done.2, bf16[32,128]{1,0:T(8,128)(2,1)S(1)} %bitcast.21, ...), custom_call_target="tpu_custom_call" | custom-call | flops 536870912 | bytes 8388608 | tf_op jit(solution)/shard_map/direct/pallas_call | solution.py:297
  25.7 0.1 compare_select_fusion.weight_ref
  25.8 6.8 %all-to-all-done = bf16[16,64,512]{2,1,0:T(8,128)(2,1)S(1)} async-done(((bf16[16,64,512]{2,1,0:T(8,128)(2,1)}), bf16[16,64,512]{2,1,0:T(8,128)(2,1)S(1)}, u32[]{:S(2)}, u32[]{:S(2)}) %all-to-all-start) | async-done | bytes 1048608 | tf_op jit(solution)/shard_map/all_to_all | solution.py:260
  32.6 3.0 %channel.1 = f32[16,16,128]{2,1,0:T(8,128)} custom-call(s32[2,64]{1,0:T(2,128)S(4)} %get-tuple-element.9.place_ref, bf16[1024,512]{1,0:T(8,128)(2,1)S(1)} %bitcast.19, bf16[8,4,128,256]{3,2,1,0:T(8,128)(2,1)S(1)} %copy.15.queries_ref, f32[8,8,128]{2,1,0:T(8,128)S(1)} %get-tuple-element.10.direct_ref, s32[8,8,128]{2,1,0:T(8,128)S(1)} %broadcast_in_dim.36.length_ref, ...), custom_call_target="tpu_custom_call" | custom-call | tf_op jit(solution)/shard_map/channel/pallas_call | solution.py:340
  35.6 6.9 %all-to-all-start.1 = ((f32[16,16,128]{2,1,0:T(8,128)}), f32[16,16,128]{2,1,0:T(8,128)S(1)}, u32[]{:S(2)}, u32[]{:S(2)}) async-start(f32[16,16,128]{2,1,0:T(8,128)} %channel.1), calls=%async_computation.1 | async-start | bytes 262144 | tf_op jit(solution)/shard_map/all_to_all | solution.py:359
  42.4 0.0 copy-start.1
  42.5 1.6 %copy-done.1 = bf16[64,16,1024]{2,1,0:T(8,128)(2,1)S(1)} copy-done((bf16[64,16,1024]{2,1,0:T(8,128)(2,1)S(1)}, bf16[64,16,1024]{2,1,0:T(8,128)(2,1)}, u32[]{:S(2)}) %copy-start.1) | copy-done | bytes 2097176
  44.0 1.1 %value.1 = (f32[16,16,128]{2,1,0:T(8,128)S(1)}, f32[16,8,128]{2,1,0:T(8,128)S(1)}) custom-call(bf16[16,64,1024]{2,1,0:T(8,128)(2,1)S(1)} %bitcast.18, bf16[32,128]{1,0:T(8,128)(2,1)S(1)} %bitcast.20), custom_call_target="tpu_custom_call" | custom-call | flops 134217728 | bytes 1048576 | tf_op jit(solution)/shard_map/value/pallas_call | solution.py:263
  45.1 5.3 %all-to-all-done.1.returned_ref = f32[16,16,128]{2,1,0:T(8,128)S(1)} async-done(((f32[16,16,128]{2,1,0:T(8,128)}), f32[16,16,128]{2,1,0:T(8,128)S(1)}, u32[]{:S(2)}, u32[]{:S(2)}) %all-to-all-start.1) | async-done | bytes 131104 | tf_op jit(solution)/shard_map/all_to_all | solution.py:359
  50.4 0.6 %finish.1 = f32[1,64]{1,0:T(1,128)} custom-call(f32[16,16,128]{2,1,0:T(8,128)S(1)} %all-to-all-done.1.returned_ref, f32[16,16,128]{2,1,0:T(8,128)S(1)} %get-tuple-element.11.factor_ref, f32[16,8,128]{2,1,0:T(8,128)S(1)} %get-tuple-element.12.first_ref), custom_call_target="tpu_custom_call" | custom-call | tf_op jit(solution)/shard_map/finish/pallas_call | solution.py:360
  (16 shorter events, 0.0 us)
Async XLA Ops:
  0.0 9.6 %copy-start.7 = (s32[8,8]{1,0:T(8,128)S(1)}, s32[8,8]{1,0:T(8,128)}, u32[]{:S(2)}) copy-start(s32[8,8]{1,0:T(8,128)} %param.15) | copy-start | bytes 772
  0.0 9.8 %copy-start.6 = (bf16[8,32,4096]{2,1,0:T(8,128)(2,1)S(1)}, bf16[8,32,4096]{2,1,0:T(8,128)(2,1)}, u32[]{:S(2)}) copy-start(bf16[8,32,4096]{2,1,0:T(8,128)(2,1)} %param.11) | copy-start | bytes 6291460
  2.2 30.3 %all-to-all-start = ((bf16[16,64,512]{2,1,0:T(8,128)(2,1)}), bf16[16,64,512]{2,1,0:T(8,128)(2,1)S(1)}, u32[]{:S(2)}, u32[]{:S(2)}) async-start(bf16[16,64,512]{2,1,0:T(8,128)(2,1)} %keys.1), calls=%async_computation | async-start | bytes 2097152 | tf_op jit(solution)/shard_map/all_to_all | solution.py:260
  12.2 3.0 %copy-start.8 = (s32[8,8]{1,0:T(8,128)S(1)}, s32[8,8]{1,0:T(8,128)}, u32[]{:S(2)}) copy-start(s32[8,8]{1,0:T(8,128)} %param.14) | copy-start | bytes 772
  12.2 3.1 %copy-start.4 = (bf16[4096]{0:T(1024)(128)(2,1)S(1)}, bf16[4096]{0:T(1024)(128)(2,1)}, u32[]{:S(2)}) copy-start(bf16[4096]{0:T(1024)(128)(2,1)} %param.16) | copy-start | bytes 24580
  12.2 3.1 %copy-start.5 = (s32[8]{0:T(128)S(1)}, s32[8]{0:T(128)}, u32[]{:S(2)}) copy-start(s32[8]{0:T(128)} %target_length.1) | copy-start | bytes 100
  15.3 3.4 %copy-start = (bf16[8,8,16,4096]{3,2,1,0:T(8,128)(2,1)S(1)}, bf16[8,8,16,4096]{3,2,1,0:T(8,128)(2,1)}, u32[]{:S(2)}) copy-start(bf16[8,8,16,4096]{3,2,1,0:T(8,128)(2,1)} %param.9) | copy-start | bytes 25165828
  18.7 1.0 %copy-start.2 = (bf16[8,32,1024]{2,1,0:T(8,128)(2,1)S(1)}, bf16[8,32,1024]{2,1,0:T(8,128)(2,1)}, u32[]{:S(2)}) copy-start(bf16[8,32,1024]{2,1,0:T(8,128)(2,1)} %states_ref.1) | copy-start | bytes 1572868
  25.7 16.7 %copy-start.3 = (bf16[4096]{0:T(1024)(128)(2,1)S(1)}, bf16[4096]{0:T(1024)(128)(2,1)}, u32[]{:S(2)}) copy-start(bf16[4096]{0:T(1024)(128)(2,1)} %param.17) | copy-start | bytes 24580
  35.6 14.8 %all-to-all-start.1 = ((f32[16,16,128]{2,1,0:T(8,128)}), f32[16,16,128]{2,1,0:T(8,128)S(1)}, u32[]{:S(2)}, u32[]{:S(2)}) async-start(f32[16,16,128]{2,1,0:T(8,128)} %channel.1), calls=%async_computation.1 | async-start | bytes 262144 | tf_op jit(solution)/shard_map/all_to_all | solution.py:359
  42.4 1.6 %copy-start.1 = (bf16[64,16,1024]{2,1,0:T(8,128)(2,1)S(1)}, bf16[64,16,1024]{2,1,0:T(8,128)(2,1)}, u32[]{:S(2)}) copy-start(bf16[64,16,1024]{2,1,0:T(8,128)(2,1)} %param.12) | copy-start | bytes 6291460

commit v5 on v4

--- a/solution.py
+++ b/solution.py
@@ -14,7 +14,7 @@
 SUBLANES = 8
 MASKED = -1e30
 PACKED = 4
-KEY_PARTS = 2
+KEY_PARTS = 4
 
 bf16 = jnp.bfloat16
 f32 = jnp.float32
@@ -337,6 +337,7 @@
     token = jnp.arange(columns, dtype=jnp.int32)[None, :] // share
     count = target_length[:, None]
     weight = jnp.where(token < count, 1.0 / count.astype(f32), 0.0)
+    direct, factor, first = lax.optimization_barrier((direct, factor, first))
     outgoing = pl.pallas_call(
         functools.partial(channel_kernel, rows),
         out_shape=jax.ShapeDtypeStruct((peers, keys, LANES), f32),

time: 51.5 us -> 50.5 us (0.981)
  blocking collectives: 0 us -> 14.6 us
  starting transfers between devices: 14.3 us -> 7.4 us
  waiting for transfers between devices: 12 us -> 5.1 us
  local copies, waits for them, and re-layouts: 11.5 us -> 10.5 us
  Pallas kernels: 12.9 us -> 12.2 us
    all_to_all x0 -> x1, blocking collectives: none -> 14.6 us  [on_device(): lax.all_to_all(outgoing, 'dp', split_axis=0, concat_axis=0, tiled=True)]
    all_to_all x1 -> x0, starting transfers between devices: 6.86 us -> none  [on_device(): lax.all_to_all(outgoing, 'dp', split_axis=0, concat_axis=0, tiled=True)]
    all_to_all x1 -> x0, waiting for transfers between devices: 5.25 us -> none  [on_device(): lax.all_to_all(outgoing, 'dp', split_axis=0, concat_axis=0, tiled=True)]
    all_to_all x1, waiting for transfers between devices: 6.75 us -> 5.1 us  [on_device(): lax.all_to_all(sent, 'dp', split_axis=0, concat_axis=0, tiled=True)]
    unnamed x19, local copies, waits for them, and re-layouts: 6.52 us -> 5.48 us
    pallas_call x1, Pallas kernels: 3.01 us -> 2.37 us  [on_device(): pl.pallas_call(functools.partial(channel_kernel, rows), out_shape=jax.Sha...]
  transfers between devices with their start and end apart: 2 -> 1, of which waited for: 2 -> 1; matrix products, arithmetic and copies ran while one was open for 11% -> 11% of each run, Pallas kernels for 14% -> 14%
where the time goes in v5:
time: 50.5 us; the launch traced here: 50.1 us
  blocking collectives  14.6 us (29%)
  Pallas kernels  12.2 us (24%)
  local copies, waits for them, and re-layouts  10.5 us (21%)
  starting transfers between devices  7.4 us (15%)
  waiting for transfers between devices  5.1 us (10%)
    all_to_all x1, blocking collectives, on_device(): lax.all_to_all(outgoing, 'dp', split_axis=0, concat_axis=0, tiled=True)  14.6 us
    all_to_all x1, starting transfers between devices, on_device(): lax.all_to_all(sent, 'dp', split_axis=0, concat_axis=0, tiled=True)  7.4 us
    pallas_call x1, Pallas kernels, on_device(): pl.pallas_call(direct_kernel, out_shape=(jax.ShapeDtypeStruct((targets, s...  6.03 us
    unnamed x19, local copies, waits for them, and re-layouts  5.48 us
    all_to_all x1, waiting for transfers between devices, on_device(): lax.all_to_all(sent, 'dp', split_axis=0, concat_axis=0, tiled=True)  5.1 us
    reshape x1, local copies, waits for them, and re-layouts, on_device(): queries.transpose(0, 2, 4, 1, 3)  2.87 us
    pallas_call x1, Pallas kernels, on_device(): pl.pallas_call(functools.partial(channel_kernel, rows), out_shape=jax.Sha...  2.37 us
    pallas_call x1, Pallas kernels, on_device(): pl.pallas_call(keys_kernel, out_shape=jax.ShapeDtypeStruct((peers, body,...  2.16 us
  transfers between devices with their start and end apart: 1, of which 1 were waited for; matrix products, arithmetic and copies ran while one was open for 11% of the time, Pallas kernels for 14%

profile of v5, /device:TPU:0, one launch (start us, length us, event | category | flops | bytes accessed | tf_op | source)
XLA Modules:
  0.0 50.1 jit_solution(4675520328547902290)
XLA Ops:
  0.0 2.2 %keys.1 = bf16[16,64,512]{2,1,0:T(8,128)(2,1)} custom-call(bf16[16,64,1024]{2,1,0:T(8,128)(2,1)} %bitcast.17), custom_call_target="tpu_custom_call" | custom-call | tf_op jit(solution)/shard_map/keys/pallas_call | solution.py:248
  2.2 7.4 %all-to-all-start = ((bf16[16,64,512]{2,1,0:T(8,128)(2,1)}), bf16[16,64,512]{2,1,0:T(8,128)(2,1)S(1)}, u32[]{:S(2)}, u32[]{:S(2)}) async-start(bf16[16,64,512]{2,1,0:T(8,128)(2,1)} %keys.1), calls=%async_computation | async-start | bytes 2097152 | tf_op jit(solution)/shard_map/all_to_all | solution.py:260
  9.6 0.0 copy-done.7
  9.6 0.1 eq.17
  9.7 0.1 mul.28
  9.8 0.0 copy-done.6
  9.8 0.5 copy.16
  10.2 1.9 %copy.18 = bf16[8,4,128,32,8]{2,4,3,1,0:T(8,128)(2,1)} copy(bf16[8,4,128,32,8]{2,4,1,3,0:T(8,128)(2,1)S(1)} %bitcast.23) | data formatting | bytes 4194304 | tf_op jit(solution)/shard_map/transpose | solution.py:334
  12.1 2.9 %copy.15.queries_ref = bf16[8,4,128,256]{3,2,1,0:T(8,128)(2,1)S(1)} copy(bf16[8,4,128,256]{2,3,1,0:T(8,128)(2,1)} %bitcast.22) | data formatting | bytes 4194304 | tf_op jit(solution)/shard_map/reshape | solution.py:334
  15.0 0.0 copy-start.5
  15.0 0.0 copy-start.1
  15.0 1.6 %copy-done.1 = bf16[64,16,1024]{2,1,0:T(8,128)(2,1)S(1)} copy-done((bf16[64,16,1024]{2,1,0:T(8,128)(2,1)S(1)}, bf16[64,16,1024]{2,1,0:T(8,128)(2,1)}, u32[]{:S(2)}) %copy-start.1) | copy-done | bytes 2097176
  16.6 1.1 %value.1 = (f32[16,16,128]{2,1,0:T(8,128)S(1)}, f32[16,8,128]{2,1,0:T(8,128)S(1)}) custom-call(bf16[16,64,1024]{2,1,0:T(8,128)(2,1)S(1)} %bitcast.18, bf16[32,128]{1,0:T(8,128)(2,1)S(1)} %bitcast.20), custom_call_target="tpu_custom_call" | custom-call | flops 134217728 | bytes 1048576 | tf_op jit(solution)/shard_map/value/pallas_call | solution.py:263
  17.7 0.1 select_reduce_fusion
  17.8 0.1 broadcast_in_dim.36.length_ref
  17.9 0.0 copy-done.2
  17.9 0.0 copy-start
  17.9 3.4 %copy-done = bf16[8,8,16,4096]{3,2,1,0:T(8,128)(2,1)S(1)} copy-done((bf16[8,8,16,4096]{3,2,1,0:T(8,128)(2,1)S(1)}, bf16[8,8,16,4096]{3,2,1,0:T(8,128)(2,1)}, u32[]{:S(2)}) %copy-start) | copy-done | bytes 8388632
  21.3 6.0 %direct.1 = (f32[8,8,128]{2,1,0:T(8,128)S(1)}, s32[2,64]{1,0:T(2,128)S(4)}) custom-call(s32[8]{0:T(128)S(1)} %copy-done.5, s32[2,64]{1,0:T(2,128)S(1)} %pad_add_fusion.at_ref, bf16[8,128,4096]{2,1,0:T(8,128)(2,1)S(1)} %bitcast.16, bf16[8,32,1024]{2,1,0:T(8,128)(2,1)S(1)} %copy-done.2, bf16[32,128]{1,0:T(8,128)(2,1)S(1)} %bitcast.21, ...), custom_call_target="tpu_custom_call" | custom-call | flops 536870912 | bytes 8388608 | tf_op jit(solution)/shard_map/direct/pallas_call | solution.py:297
  27.3 0.1 compare_select_fusion.weight_ref
  27.4 5.1 %all-to-all-done = bf16[16,64,512]{2,1,0:T(8,128)(2,1)S(1)} async-done(((bf16[16,64,512]{2,1,0:T(8,128)(2,1)}), bf16[16,64,512]{2,1,0:T(8,128)(2,1)S(1)}, u32[]{:S(2)}, u32[]{:S(2)}) %all-to-all-start) | async-done | bytes 1048608 | tf_op jit(solution)/shard_map/all_to_all | solution.py:260
  32.5 2.4 %channel.1 = f32[16,16,128]{2,1,0:T(8,128)S(1)} custom-call(s32[2,64]{1,0:T(2,128)S(4)} %get-tuple-element.12.place_ref, bf16[1024,512]{1,0:T(8,128)(2,1)S(1)} %bitcast.19, bf16[8,4,128,256]{3,2,1,0:T(8,128)(2,1)S(1)} %copy.15.queries_ref, f32[8,8,128]{2,1,0:T(8,128)S(1)} %get-tuple-element.16.direct_ref, s32[8,8,128]{2,1,0:T(8,128)S(1)} %broadcast_in_dim.36.length_ref, ...), custom_call_target="tpu_custom_call" | custom-call | tf_op jit(solution)/shard_map/channel/pallas_call | solution.py:341
  34.9 14.6 %all_to_all.10.returned_ref = f32[16,16,128]{2,1,0:T(8,128)S(1)} all-to-all(f32[16,16,128]{2,1,0:T(8,128)S(1)} %channel.1), channel_id=1, replica_groups=mesh['group'=2,'dp'=16] {'dp'}, dimensions={0} | all-to-all | bytes 262144 | tf_op jit(solution)/shard_map/all_to_all | solution.py:360
  49.5 0.6 %finish.1 = f32[1,64]{1,0:T(1,128)} custom-call(f32[16,16,128]{2,1,0:T(8,128)S(1)} %all_to_all.10.returned_ref, f32[16,16,128]{2,1,0:T(8,128)S(1)} %get-tuple-element.17.factor_ref, f32[16,8,128]{2,1,0:T(8,128)S(1)} %get-tuple-element.18.first_ref), custom_call_target="tpu_custom_call" | custom-call | tf_op jit(solution)/shard_map/finish/pallas_call | solution.py:361
  (15 shorter events, 0.0 us)
Async XLA Ops:
  0.0 9.6 %copy-start.7 = (s32[8,8]{1,0:T(8,128)S(1)}, s32[8,8]{1,0:T(8,128)}, u32[]{:S(2)}) copy-start(s32[8,8]{1,0:T(8,128)} %param.15) | copy-start | bytes 772
  0.0 9.8 %copy-start.6 = (bf16[8,32,4096]{2,1,0:T(8,128)(2,1)S(1)}, bf16[8,32,4096]{2,1,0:T(8,128)(2,1)}, u32[]{:S(2)}) copy-start(bf16[8,32,4096]{2,1,0:T(8,128)(2,1)} %param.11) | copy-start | bytes 6291460
  2.2 30.3 %all-to-all-start = ((bf16[16,64,512]{2,1,0:T(8,128)(2,1)}), bf16[16,64,512]{2,1,0:T(8,128)(2,1)S(1)}, u32[]{:S(2)}, u32[]{:S(2)}) async-start(bf16[16,64,512]{2,1,0:T(8,128)(2,1)} %keys.1), calls=%async_computation | async-start | bytes 2097152 | tf_op jit(solution)/shard_map/all_to_all | solution.py:260
  12.1 2.9 %copy-start.3 = (bf16[4096]{0:T(1024)(128)(2,1)S(1)}, bf16[4096]{0:T(1024)(128)(2,1)}, u32[]{:S(2)}) copy-start(bf16[4096]{0:T(1024)(128)(2,1)} %param.17) | copy-start | bytes 24580
  15.0 2.9 %copy-start.5 = (s32[8]{0:T(128)S(1)}, s32[8]{0:T(128)}, u32[]{:S(2)}) copy-start(s32[8]{0:T(128)} %target_length.1) | copy-start | bytes 100
  15.0 1.6 %copy-start.1 = (bf16[64,16,1024]{2,1,0:T(8,128)(2,1)S(1)}, bf16[64,16,1024]{2,1,0:T(8,128)(2,1)}, u32[]{:S(2)}) copy-start(bf16[64,16,1024]{2,1,0:T(8,128)(2,1)} %param.12) | copy-start | bytes 6291460
  16.6 1.2 %copy-start.8 = (s32[8,8]{1,0:T(8,128)S(1)}, s32[8,8]{1,0:T(8,128)}, u32[]{:S(2)}) copy-start(s32[8,8]{1,0:T(8,128)} %param.14) | copy-start | bytes 772
  16.6 1.3 %copy-start.2 = (bf16[8,32,1024]{2,1,0:T(8,128)(2,1)S(1)}, bf16[8,32,1024]{2,1,0:T(8,128)(2,1)}, u32[]{:S(2)}) copy-start(bf16[8,32,1024]{2,1,0:T(8,128)(2,1)} %states_ref.1) | copy-start | bytes 1572868
  16.6 1.3 %copy-start.4 = (bf16[4096]{0:T(1024)(128)(2,1)S(1)}, bf16[4096]{0:T(1024)(128)(2,1)}, u32[]{:S(2)}) copy-start(bf16[4096]{0:T(1024)(128)(2,1)} %param.16) | copy-start | bytes 24580
  17.9 3.4 %copy-start = (bf16[8,8,16,4096]{3,2,1,0:T(8,128)(2,1)S(1)}, bf16[8,8,16,4096]{3,2,1,0:T(8,128)(2,1)}, u32[]{:S(2)}) copy-start(bf16[8,8,16,4096]{3,2,1,0:T(8,128)(2,1)} %param.9) | copy-start | bytes 25165828

commit v6 on v5

--- a/solution.py
+++ b/solution.py
@@ -15,11 +15,21 @@
 MASKED = -1e30
 PACKED = 4
 KEY_PARTS = 4
+OUT_FLIP = 3
+BACK_FLIP = 3
 
 bf16 = jnp.bfloat16
 f32 = jnp.float32
 
 
+def turned(i, count, flip):
+    return ((i + count // 2) % count) ^ flip
+
+
+def place_of(device, count, flip):
+    return ((device ^ flip) + count // 2) % count
+
+
 def dot_nt(a, b):
     return lax.dot_general(a, b, (((1,), (1,)), ((), ())), preferred_element_type=f32)
 
@@ -34,7 +44,7 @@
 
 def keys_kernel(states_ref, out_ref, held_ref, sems):
     peers, _, width = out_ref.shape
-    parts = sems.shape[1]
+    parts = KEY_PARTS
     step = peers // parts
     loads, sends = [], []
     for i in range(parts):
@@ -42,11 +52,16 @@
         loads.append(
             pltpu.make_async_copy(states_ref.at[at, :, :width], held_ref.at[at], sems.at[0, i])
         )
-        sends.append(pltpu.make_async_copy(held_ref.at[at], out_ref.at[at], sems.at[1, i]))
         loads[i].start()
     for i in range(parts):
         loads[i].wait()
-        sends[i].start()
+        size = step if OUT_FLIP == 0 else 1
+        for j in range(i * step, (i + 1) * step, size):
+            to = pl.ds(place_of(j, peers, OUT_FLIP), size)
+            sends.append(
+                pltpu.make_async_copy(held_ref.at[j : j + size], out_ref.at[to], sems.at[1, j // size])
+            )
+            sends[-1].start()
     for copy in sends:
         copy.wait()
 
@@ -72,14 +87,15 @@
         factor_ref[...] = jnp.zeros_like(factor_ref)
     first_ref[...] = jnp.zeros_like(first_ref)
     for p in range(peers):
+        to = p ^ BACK_FLIP
         for r in range(rows):
             start = p * body + r * keys
             value = read_ref[pl.ds(start, PACKED, stride=PACKED), :]
             for i in range(1, PACKED):
                 value = jnp.where(part == i, read_ref[pl.ds(start + i, PACKED, stride=PACKED), :], value)
             first = read_ref[start : start + 1, :]
-            factor_ref[p, pl.ds(r, PACKED, stride=PACKED), :] = jnp.where(first_key, 1.0, value - first)
-            first_ref[p, r : r + 1, :] = jnp.where(part[:1] == 0, first, 0.0)
+            factor_ref[to, pl.ds(r, PACKED, stride=PACKED), :] = jnp.where(first_key, 1.0, value - first)
+            first_ref[to, r : r + 1, :] = jnp.where(part[:1] == 0, first, 0.0)
 
 
 def direct_kernel(
@@ -198,9 +214,10 @@
             pooled_ref[start : start + slots, :] = part
     if rows < PACKED:
         out_ref[...] = jnp.zeros_like(out_ref)
-    for p in range(peers):
+    for i in range(peers):
+        p = turned(i, peers, BACK_FLIP)
         for r in range(rows):
-            out_ref[p, pl.ds(r, PACKED, stride=PACKED), :] = pooled_ref[
+            out_ref[i, pl.ds(r, PACKED, stride=PACKED), :] = pooled_ref[
                 pl.ds(place_ref[1, p * rows + r], PACKED, stride=slots), :
             ]
 
@@ -210,7 +227,7 @@
     total = total[:, :SUBLANES] + total[:, SUBLANES:] + first_ref[...]
     total = jnp.sum(total, axis=2, keepdims=True)
     shape = (total.shape[0], SUBLANES, LANES)
-    at = iota(shape, 0) * rows + iota(shape, 1) % PACKED
+    at = turned(iota(shape, 0), shape[0], BACK_FLIP) * rows + iota(shape, 1) % PACKED
     total = jnp.where((iota(shape, 2) == at) & (iota(shape, 1) % PACKED < rows), total, 0.0)
     total = jnp.sum(jnp.sum(total, axis=0), axis=0, keepdims=True)
     out_ref[...] = total[:, : out_ref.shape[1]]
@@ -252,14 +269,19 @@
         out_specs=hbm,
         scratch_shapes=[
             pltpu.VMEM((peers, body, width), bf16),
-            pltpu.SemaphoreType.DMA((2, KEY_PARTS)),
+            pltpu.SemaphoreType.DMA((2, KEY_PARTS if OUT_FLIP == 0 else peers)),
         ],
         compiler_params=pltpu.CompilerParams(vmem_limit_bytes=16 * 2**20),
         name="keys",
     )(pltpu.with_memory_space_constraint(candidate_states.reshape(peers, body, 2 * width), pltpu.HBM))
-    arrived = lax.all_to_all(sent, "dp", split_axis=0, concat_axis=0, tiled=True)
-
-    step = max(1, peers // 4)
+    assert peers % 16 == 0
+    out_order = [turned(i, peers, OUT_FLIP) for i in range(peers)]
+    back_order = [turned(i, peers, BACK_FLIP) for i in range(peers)]
+    exchange = functools.partial(lax.all_to_all, axis_name="dp", split_axis=0, concat_axis=0, tiled=True)
+    arrived = exchange(sent, axis_index_groups=[out_order])
+
+    step = peers // 4
+    half = 2
     factor, first = pl.pallas_call(
         functools.partial(value_kernel, rows, keys),
         out_shape=(
@@ -272,8 +294,8 @@
             pl.BlockSpec((heads, HEAD_SIZE), lambda i: (0, 0)),
         ],
         out_specs=(
-            pl.BlockSpec((step, keys, LANES), lambda i: (i, 0, 0)),
-            pl.BlockSpec((step, SUBLANES, LANES), lambda i: (i, 0, 0)),
+            pl.BlockSpec((step, keys, LANES), lambda i: ((i + half) % (2 * half), 0, 0)),
+            pl.BlockSpec((step, SUBLANES, LANES), lambda i: ((i + half) % (2 * half), 0, 0)),
         ),
         scratch_shapes=[pltpu.VMEM((step * body, LANES), f32)],
         compiler_params=pltpu.CompilerParams(vmem_limit_bytes=16 * 2**20),
@@ -293,7 +315,8 @@
     pair = jnp.arange(candidates, dtype=jnp.int32)
     start = pair // slots * (slots * PACKED) + pair % slots
     start = jnp.sum(jnp.where(flat[None, :] == pair[:, None], start[None, :], 0), axis=1)
-    at = jnp.stack([flat * keys, start])
+    held = place_of(flat // rows, peers, OUT_FLIP) * body + flat % rows * keys
+    at = jnp.stack([held, start])
     direct, place = pl.pallas_call(
         direct_kernel,
         out_shape=(
@@ -357,7 +380,7 @@
         length_lanes,
         weight,
     )
-    returned = lax.all_to_all(outgoing, "dp", split_axis=0, concat_axis=0, tiled=True)
+    returned = exchange(outgoing, axis_index_groups=[back_order])
     result = pl.pallas_call(
         functools.partial(finish_kernel, rows),
         out_shape=jax.ShapeDtypeStruct((1, candidates), f32),

time: 50.5 us -> 45.8 us (0.907)
  blocking collectives: 14.6 us -> 11 us
  waiting for transfers between devices: 5.1 us -> 2.92 us
  starting transfers between devices: 7.4 us -> 7.98 us
    all_to_all x1, blocking collectives: 14.6 us -> 11 us  [on_device(): returned = exchange(outgoing, axis_index_groups=[back_order])]
    all_to_all x1, waiting for transfers between devices: 5.1 us -> 2.92 us  [on_device(): arrived = exchange(sent, axis_index_groups=[out_order])]
    all_to_all x1, starting transfers between devices: 7.4 us -> 7.98 us  [on_device(): arrived = exchange(sent, axis_index_groups=[out_order])]
  transfers between devices with their start and end apart: 1 -> 1, of which waited for: 1 -> 1; matrix products, arithmetic and copies ran while one was open for 11% -> 13% of each run, Pallas kernels for 14% -> 16%
where the time goes in v6:
time: 45.8 us; the launch traced here: 45.2 us
  Pallas kernels  12.5 us (27%)
  blocking collectives  11 us (24%)
  local copies, waits for them, and re-layouts  10.4 us (23%)
  starting transfers between devices  7.98 us (17%)
  waiting for transfers between devices  2.92 us (6%)
    all_to_all x1, blocking collectives, on_device(): returned = exchange(outgoing, axis_index_groups=[back_order])  11 us
    all_to_all x1, starting transfers between devices, on_device(): arrived = exchange(sent, axis_index_groups=[out_order])  7.98 us
    pallas_call x1, Pallas kernels, on_device(): pl.pallas_call(direct_kernel, out_shape=(jax.ShapeDtypeStruct((targets, s...  6.02 us
    unnamed x19, local copies, waits for them, and re-layouts  5.48 us
    all_to_all x1, waiting for transfers between devices, on_device(): arrived = exchange(sent, axis_index_groups=[out_order])  2.92 us
    reshape x1, local copies, waits for them, and re-layouts, on_device(): queries.transpose(0, 2, 4, 1, 3)  2.87 us
    pallas_call x1, Pallas kernels, on_device(): pl.pallas_call(keys_kernel, out_shape=jax.ShapeDtypeStruct((peers, body,...  2.4 us
    pallas_call x1, Pallas kernels, on_device(): pl.pallas_call(functools.partial(channel_kernel, rows), out_shape=jax.Sha...  2.38 us
  transfers between devices with their start and end apart: 1, of which 1 were waited for; matrix products, arithmetic and copies ran while one was open for 13% of the time, Pallas kernels for 16%

profile of v6, /device:TPU:0, one launch (start us, length us, event | category | flops | bytes accessed | tf_op | source)
XLA Modules:
  0.0 45.2 jit_solution(7657969468607305458)
XLA Ops:
  0.0 2.4 %keys.1 = bf16[16,64,512]{2,1,0:T(8,128)(2,1)} custom-call(bf16[16,64,1024]{2,1,0:T(8,128)(2,1)} %bitcast.17), custom_call_target="tpu_custom_call" | custom-call | tf_op jit(solution)/shard_map/keys/pallas_call | solution.py:265
  2.4 8.0 %all-to-all-start = ((bf16[16,64,512]{2,1,0:T(8,128)(2,1)}), bf16[16,64,512]{2,1,0:T(8,128)(2,1)S(1)}, u32[]{:S(2)}, u32[]{:S(2)}) async-start(bf16[16,64,512]{2,1,0:T(8,128)(2,1)} %keys.1), calls=%async_computation | async-start | bytes 2097152 | tf_op jit(solution)/shard_map/all_to_all | solution.py:281
  10.4 0.1 eq.19
  10.5 0.1 reshape.236
  10.6 0.0 copy-done.6
  10.6 0.5 %copy.16 = bf16[32,8,32,128]{3,2,1,0:T(8,128)(2,1)S(1)} copy(bf16[32,8,32,128]{3,1,2,0:T(8,128)(2,1)S(1)} %bitcast.24) | data formatting | bytes 4194304
  11.1 1.9 %copy.18 = bf16[8,4,128,32,8]{2,4,3,1,0:T(8,128)(2,1)} copy(bf16[8,4,128,32,8]{2,4,1,3,0:T(8,128)(2,1)S(1)} %bitcast.23) | data formatting | bytes 4194304 | tf_op jit(solution)/shard_map/transpose | solution.py:357
  12.9 2.9 %copy.15.queries_ref = bf16[8,4,128,256]{3,2,1,0:T(8,128)(2,1)S(1)} copy(bf16[8,4,128,256]{2,3,1,0:T(8,128)(2,1)} %bitcast.22) | data formatting | bytes 4194304 | tf_op jit(solution)/shard_map/reshape | solution.py:357
  15.8 0.0 copy-start.5
  15.8 0.0 copy-start.1
  15.8 1.6 %copy-done.1 = bf16[64,16,1024]{2,1,0:T(8,128)(2,1)S(1)} copy-done((bf16[64,16,1024]{2,1,0:T(8,128)(2,1)S(1)}, bf16[64,16,1024]{2,1,0:T(8,128)(2,1)}, u32[]{:S(2)}) %copy-start.1) | copy-done | bytes 2097176
  17.4 1.1 %value.1 = (f32[16,16,128]{2,1,0:T(8,128)S(1)}, f32[16,8,128]{2,1,0:T(8,128)S(1)}) custom-call(bf16[16,64,1024]{2,1,0:T(8,128)(2,1)S(1)} %bitcast.18, bf16[32,128]{1,0:T(8,128)(2,1)S(1)} %bitcast.20), custom_call_target="tpu_custom_call" | custom-call | flops 134217728 | bytes 1048576 | tf_op jit(solution)/shard_map/value/pallas_call | solution.py:285
  18.5 0.1 select_reduce_fusion
  18.7 0.1 broadcast_in_dim.36.length_ref
  18.8 0.0 copy-done.5
  18.8 0.0 copy-done.4
  18.8 0.0 copy-start
  18.8 3.4 %copy-done = bf16[8,8,16,4096]{3,2,1,0:T(8,128)(2,1)S(1)} copy-done((bf16[8,8,16,4096]{3,2,1,0:T(8,128)(2,1)S(1)}, bf16[8,8,16,4096]{3,2,1,0:T(8,128)(2,1)}, u32[]{:S(2)}) %copy-start) | copy-done | bytes 8388632
  22.2 6.0 %direct.1 = (f32[8,8,128]{2,1,0:T(8,128)S(1)}, s32[2,64]{1,0:T(2,128)S(4)}) custom-call(s32[8]{0:T(128)S(1)} %copy-done.5, s32[2,64]{1,0:T(2,128)S(1)} %pad_add_fusion.at_ref, bf16[8,128,4096]{2,1,0:T(8,128)(2,1)S(1)} %bitcast.16, bf16[8,32,1024]{2,1,0:T(8,128)(2,1)S(1)} %copy-done.2, bf16[32,128]{1,0:T(8,128)(2,1)S(1)} %bitcast.21, ...), custom_call_target="tpu_custom_call" | custom-call | flops 536870912 | bytes 8388608 | tf_op jit(solution)/shard_map/direct/pallas_call | solution.py:320
  28.2 0.1 compare_select_fusion.weight_ref
  28.3 2.9 %all-to-all-done = bf16[16,64,512]{2,1,0:T(8,128)(2,1)S(1)} async-done(((bf16[16,64,512]{2,1,0:T(8,128)(2,1)}), bf16[16,64,512]{2,1,0:T(8,128)(2,1)S(1)}, u32[]{:S(2)}, u32[]{:S(2)}) %all-to-all-start) | async-done | bytes 1048608 | tf_op jit(solution)/shard_map/all_to_all | solution.py:281
  31.2 2.4 %channel.1 = f32[16,16,128]{2,1,0:T(8,128)S(1)} custom-call(s32[2,64]{1,0:T(2,128)S(4)} %get-tuple-element.12.place_ref, bf16[1024,512]{1,0:T(8,128)(2,1)S(1)} %bitcast.19, bf16[8,4,128,256]{3,2,1,0:T(8,128)(2,1)S(1)} %copy.15.queries_ref, f32[8,8,128]{2,1,0:T(8,128)S(1)} %get-tuple-element.16.direct_ref, s32[8,8,128]{2,1,0:T(8,128)S(1)} %broadcast_in_dim.36.length_ref, ...), custom_call_target="tpu_custom_call" | custom-call | tf_op jit(solution)/shard_map/channel/pallas_call | solution.py:364
  33.6 11.0 %all_to_all.10.returned_ref = f32[16,16,128]{2,1,0:T(8,128)S(1)} all-to-all(f32[16,16,128]{2,1,0:T(8,128)S(1)} %channel.1), channel_id=1, replica_groups={{11,10,9,8,15,14,13,12,3,2,1,0,7,6,5,4},{27,26,25,24,31,30,29,28,19,18,..., dimensions={0} | all-to-all | bytes 262144 | tf_op jit(solution)/shard_map/all_to_all | solution.py:383
  44.6 0.6 %finish.1 = f32[1,64]{1,0:T(1,128)} custom-call(f32[16,16,128]{2,1,0:T(8,128)S(1)} %all_to_all.10.returned_ref, f32[16,16,128]{2,1,0:T(8,128)S(1)} %get-tuple-element.17.factor_ref, f32[16,8,128]{2,1,0:T(8,128)S(1)} %get-tuple-element.18.first_ref), custom_call_target="tpu_custom_call" | custom-call | tf_op jit(solution)/shard_map/finish/pallas_call | solution.py:384
  (15 shorter events, 0.1 us)
Async XLA Ops:
  0.0 10.4 %copy-start.7 = (s32[8,8]{1,0:T(8,128)S(1)}, s32[8,8]{1,0:T(8,128)}, u32[]{:S(2)}) copy-start(s32[8,8]{1,0:T(8,128)} %param.15) | copy-start | bytes 772
  0.0 10.6 %copy-start.6 = (bf16[8,32,4096]{2,1,0:T(8,128)(2,1)S(1)}, bf16[8,32,4096]{2,1,0:T(8,128)(2,1)}, u32[]{:S(2)}) copy-start(bf16[8,32,4096]{2,1,0:T(8,128)(2,1)} %param.11) | copy-start | bytes 6291460
  2.4 28.8 %all-to-all-start = ((bf16[16,64,512]{2,1,0:T(8,128)(2,1)}), bf16[16,64,512]{2,1,0:T(8,128)(2,1)S(1)}, u32[]{:S(2)}, u32[]{:S(2)}) async-start(bf16[16,64,512]{2,1,0:T(8,128)(2,1)} %keys.1), calls=%async_computation | async-start | bytes 2097152 | tf_op jit(solution)/shard_map/all_to_all | solution.py:281
  12.9 2.9 %copy-start.3 = (bf16[4096]{0:T(1024)(128)(2,1)S(1)}, bf16[4096]{0:T(1024)(128)(2,1)}, u32[]{:S(2)}) copy-start(bf16[4096]{0:T(1024)(128)(2,1)} %param.17) | copy-start | bytes 24580
  15.8 2.9 %copy-start.5 = (s32[8]{0:T(128)S(1)}, s32[8]{0:T(128)}, u32[]{:S(2)}) copy-start(s32[8]{0:T(128)} %target_length.1) | copy-start | bytes 100
  15.8 1.6 %copy-start.1 = (bf16[64,16,1024]{2,1,0:T(8,128)(2,1)S(1)}, bf16[64,16,1024]{2,1,0:T(8,128)(2,1)}, u32[]{:S(2)}) copy-start(bf16[64,16,1024]{2,1,0:T(8,128)(2,1)} %param.12) | copy-start | bytes 6291460
  17.4 1.2 %copy-start.8 = (s32[8,8]{1,0:T(8,128)S(1)}, s32[8,8]{1,0:T(8,128)}, u32[]{:S(2)}) copy-start(s32[8,8]{1,0:T(8,128)} %param.14) | copy-start | bytes 772
  17.4 1.3 %copy-start.2 = (bf16[8,32,1024]{2,1,0:T(8,128)(2,1)S(1)}, bf16[8,32,1024]{2,1,0:T(8,128)(2,1)}, u32[]{:S(2)}) copy-start(bf16[8,32,1024]{2,1,0:T(8,128)(2,1)} %states_ref.1) | copy-start | bytes 1572868
  17.4 1.3 %copy-start.4 = (bf16[4096]{0:T(1024)(128)(2,1)S(1)}, bf16[4096]{0:T(1024)(128)(2,1)}, u32[]{:S(2)}) copy-start(bf16[4096]{0:T(1024)(128)(2,1)} %param.16) | copy-start | bytes 24580
  18.8 3.4 %copy-start = (bf16[8,8,16,4096]{3,2,1,0:T(8,128)(2,1)S(1)}, bf16[8,8,16,4096]{3,2,1,0:T(8,128)(2,1)}, u32[]{:S(2)}) copy-start(bf16[8,8,16,4096]{3,2,1,0:T(8,128)(2,1)} %param.9) | copy-start | bytes 25165828

commit v7 on v6

--- a/solution.py
+++ b/solution.py
@@ -30,6 +30,11 @@
     return ((device ^ flip) + count // 2) % count
 
 
+def mirrored(i, count):
+    quarter = count // 4
+    return (2 - i // quarter) % 4 * quarter + i % quarter
+
+
 def dot_nt(a, b):
     return lax.dot_general(a, b, (((1,), (1,)), ((), ())), preferred_element_type=f32)
 
@@ -57,7 +62,7 @@
         loads[i].wait()
         size = step if OUT_FLIP == 0 else 1
         for j in range(i * step, (i + 1) * step, size):
-            to = pl.ds(place_of(j, peers, OUT_FLIP), size)
+            to = pl.ds(mirrored(j ^ OUT_FLIP, peers), size)
             sends.append(
                 pltpu.make_async_copy(held_ref.at[j : j + size], out_ref.at[to], sems.at[1, j // size])
             )
@@ -275,7 +280,7 @@
         name="keys",
     )(pltpu.with_memory_space_constraint(candidate_states.reshape(peers, body, 2 * width), pltpu.HBM))
     assert peers % 16 == 0
-    out_order = [turned(i, peers, OUT_FLIP) for i in range(peers)]
+    out_order = [mirrored(i, peers) ^ OUT_FLIP for i in range(peers)]
     back_order = [turned(i, peers, BACK_FLIP) for i in range(peers)]
     exchange = functools.partial(lax.all_to_all, axis_name="dp", split_axis=0, concat_axis=0, tiled=True)
     arrived = exchange(sent, axis_index_groups=[out_order])
@@ -315,7 +320,7 @@
     pair = jnp.arange(candidates, dtype=jnp.int32)
     start = pair // slots * (slots * PACKED) + pair % slots
     start = jnp.sum(jnp.where(flat[None, :] == pair[:, None], start[None, :], 0), axis=1)
-    held = place_of(flat // rows, peers, OUT_FLIP) * body + flat % rows * keys
+    held = mirrored(flat // rows ^ OUT_FLIP, peers) * body + flat % rows * keys
     at = jnp.stack([held, start])
     direct, place = pl.pallas_call(
         direct_kernel,

time: 45.8 us -> 45.5 us (level)
  blocking collectives: 11 us -> 8.29 us
  waiting for transfers between devices: 2.92 us -> 5.39 us
    all_to_all x1, blocking collectives: 11 us -> 8.29 us  [on_device(): returned = exchange(outgoing, axis_index_groups=[back_order])]
    all_to_all x1, waiting for transfers between devices: 2.92 us -> 5.39 us  [on_device(): arrived = exchange(sent, axis_index_groups=[out_order])]
where the time goes in v7:
time: 45.5 us; the launch traced here: 44.9 us
  Pallas kernels  12.5 us (27%)
  local copies, waits for them, and re-layouts  10.4 us (23%)
  blocking collectives  8.29 us (18%)
  starting transfers between devices  7.98 us (18%)
  waiting for transfers between devices  5.39 us (12%)
    all_to_all x1, blocking collectives, on_device(): returned = exchange(outgoing, axis_index_groups=[back_order])  8.29 us
    all_to_all x1, starting transfers between devices, on_device(): arrived = exchange(sent, axis_index_groups=[out_order])  7.98 us
    pallas_call x1, Pallas kernels, on_device(): pl.pallas_call(direct_kernel, out_shape=(jax.ShapeDtypeStruct((targets, s...  6.02 us
    unnamed x19, local copies, waits for them, and re-layouts  5.48 us
    all_to_all x1, waiting for transfers between devices, on_device(): arrived = exchange(sent, axis_index_groups=[out_order])  5.39 us
    reshape x1, local copies, waits for them, and re-layouts, on_device(): queries.transpose(0, 2, 4, 1, 3)  2.87 us
    pallas_call x1, Pallas kernels, on_device(): pl.pallas_call(keys_kernel, out_shape=jax.ShapeDtypeStruct((peers, body,...  2.39 us
    pallas_call x1, Pallas kernels, on_device(): pl.pallas_call(functools.partial(channel_kernel, rows), out_shape=jax.Sha...  2.37 us
  transfers between devices with their start and end apart: 1, of which 1 were waited for; matrix products, arithmetic and copies ran while one was open for 13% of the time, Pallas kernels for 16%

profile of v7, /device:TPU:0, one launch (start us, length us, event | category | flops | bytes accessed | tf_op | source)
XLA Modules:
  0.0 44.9 jit_solution(544103465853341102)
XLA Ops:
  0.0 2.4 %keys.1 = bf16[16,64,512]{2,1,0:T(8,128)(2,1)} custom-call(bf16[16,64,1024]{2,1,0:T(8,128)(2,1)} %bitcast.17), custom_call_target="tpu_custom_call" | custom-call | tf_op jit(solution)/shard_map/keys/pallas_call | solution.py:270
  2.4 8.0 %all-to-all-start = ((bf16[16,64,512]{2,1,0:T(8,128)(2,1)}), bf16[16,64,512]{2,1,0:T(8,128)(2,1)S(1)}, u32[]{:S(2)}, u32[]{:S(2)}) async-start(bf16[16,64,512]{2,1,0:T(8,128)(2,1)} %keys.1), calls=%async_computation | async-start | bytes 2097152 | tf_op jit(solution)/shard_map/all_to_all | solution.py:286
  10.4 0.0 copy-done.7
  10.4 0.1 eq.20
  10.5 0.1 reshape.306
  10.5 0.5 %copy.16 = bf16[32,8,32,128]{3,2,1,0:T(8,128)(2,1)S(1)} copy(bf16[32,8,32,128]{3,1,2,0:T(8,128)(2,1)S(1)} %bitcast.24) | data formatting | bytes 4194304
  11.0 1.9 %copy.18 = bf16[8,4,128,32,8]{2,4,3,1,0:T(8,128)(2,1)} copy(bf16[8,4,128,32,8]{2,4,1,3,0:T(8,128)(2,1)S(1)} %bitcast.23) | data formatting | bytes 4194304 | tf_op jit(solution)/shard_map/transpose | solution.py:362
  12.9 2.9 %copy.15.queries_ref = bf16[8,4,128,256]{3,2,1,0:T(8,128)(2,1)S(1)} copy(bf16[8,4,128,256]{2,3,1,0:T(8,128)(2,1)} %bitcast.22) | data formatting | bytes 4194304 | tf_op jit(solution)/shard_map/reshape | solution.py:362
  15.8 0.0 copy-start.5
  15.8 0.0 copy-start.1
  15.8 1.6 %copy-done.1 = bf16[64,16,1024]{2,1,0:T(8,128)(2,1)S(1)} copy-done((bf16[64,16,1024]{2,1,0:T(8,128)(2,1)S(1)}, bf16[64,16,1024]{2,1,0:T(8,128)(2,1)}, u32[]{:S(2)}) %copy-start.1) | copy-done | bytes 2097176
  17.4 1.1 %value.1 = (f32[16,16,128]{2,1,0:T(8,128)S(1)}, f32[16,8,128]{2,1,0:T(8,128)S(1)}) custom-call(bf16[16,64,1024]{2,1,0:T(8,128)(2,1)S(1)} %bitcast.18, bf16[32,128]{1,0:T(8,128)(2,1)S(1)} %bitcast.20), custom_call_target="tpu_custom_call" | custom-call | flops 134217728 | bytes 1048576 | tf_op jit(solution)/shard_map/value/pallas_call | solution.py:290
  18.5 0.1 select_reduce_fusion
  18.7 0.0 copy-done.8
  18.7 0.1 broadcast_in_dim.36.length_ref
  18.7 0.0 copy-done.2
  18.8 0.0 copy-start
  18.8 3.4 %copy-done = bf16[8,8,16,4096]{3,2,1,0:T(8,128)(2,1)S(1)} copy-done((bf16[8,8,16,4096]{3,2,1,0:T(8,128)(2,1)S(1)}, bf16[8,8,16,4096]{3,2,1,0:T(8,128)(2,1)}, u32[]{:S(2)}) %copy-start) | copy-done | bytes 8388632
  22.1 6.0 %direct.1 = (f32[8,8,128]{2,1,0:T(8,128)S(1)}, s32[2,64]{1,0:T(2,128)S(4)}) custom-call(s32[8]{0:T(128)S(1)} %copy-done.5, s32[2,64]{1,0:T(2,128)S(1)} %pad_add_fusion.at_ref, bf16[8,128,4096]{2,1,0:T(8,128)(2,1)S(1)} %bitcast.16, bf16[8,32,1024]{2,1,0:T(8,128)(2,1)S(1)} %copy-done.2, bf16[32,128]{1,0:T(8,128)(2,1)S(1)} %bitcast.21, ...), custom_call_target="tpu_custom_call" | custom-call | flops 536870912 | bytes 8388608 | tf_op jit(solution)/shard_map/direct/pallas_call | solution.py:325
  28.2 0.1 compare_select_fusion.weight_ref
  28.3 5.4 %all-to-all-done = bf16[16,64,512]{2,1,0:T(8,128)(2,1)S(1)} async-done(((bf16[16,64,512]{2,1,0:T(8,128)(2,1)}), bf16[16,64,512]{2,1,0:T(8,128)(2,1)S(1)}, u32[]{:S(2)}, u32[]{:S(2)}) %all-to-all-start) | async-done | bytes 1048608 | tf_op jit(solution)/shard_map/all_to_all | solution.py:286
  33.6 2.4 %channel.1 = f32[16,16,128]{2,1,0:T(8,128)S(1)} custom-call(s32[2,64]{1,0:T(2,128)S(4)} %get-tuple-element.12.place_ref, bf16[1024,512]{1,0:T(8,128)(2,1)S(1)} %bitcast.19, bf16[8,4,128,256]{3,2,1,0:T(8,128)(2,1)S(1)} %copy.15.queries_ref, f32[8,8,128]{2,1,0:T(8,128)S(1)} %get-tuple-element.16.direct_ref, s32[8,8,128]{2,1,0:T(8,128)S(1)} %broadcast_in_dim.36.length_ref, ...), custom_call_target="tpu_custom_call" | custom-call | tf_op jit(solution)/shard_map/channel/pallas_call | solution.py:369
  36.0 8.3 %all_to_all.10.returned_ref = f32[16,16,128]{2,1,0:T(8,128)S(1)} all-to-all(f32[16,16,128]{2,1,0:T(8,128)S(1)} %channel.1), channel_id=1, replica_groups={{11,10,9,8,15,14,13,12,3,2,1,0,7,6,5,4},{27,26,25,24,31,30,29,28,19,18,..., dimensions={0} | all-to-all | bytes 262144 | tf_op jit(solution)/shard_map/all_to_all | solution.py:388
  44.3 0.6 %finish.1 = f32[1,64]{1,0:T(1,128)} custom-call(f32[16,16,128]{2,1,0:T(8,128)S(1)} %all_to_all.10.returned_ref, f32[16,16,128]{2,1,0:T(8,128)S(1)} %get-tuple-element.17.factor_ref, f32[16,8,128]{2,1,0:T(8,128)S(1)} %get-tuple-element.18.first_ref), custom_call_target="tpu_custom_call" | custom-call | tf_op jit(solution)/shard_map/finish/pallas_call | solution.py:389
  (15 shorter events, 0.1 us)
Async XLA Ops:
  0.0 10.4 %copy-start.7 = (s32[8,8]{1,0:T(8,128)S(1)}, s32[8,8]{1,0:T(8,128)}, u32[]{:S(2)}) copy-start(s32[8,8]{1,0:T(8,128)} %param.15) | copy-start | bytes 772
  0.0 10.5 %copy-start.6 = (bf16[8,32,4096]{2,1,0:T(8,128)(2,1)S(1)}, bf16[8,32,4096]{2,1,0:T(8,128)(2,1)}, u32[]{:S(2)}) copy-start(bf16[8,32,4096]{2,1,0:T(8,128)(2,1)} %param.11) | copy-start | bytes 6291460
  2.4 31.2 %all-to-all-start = ((bf16[16,64,512]{2,1,0:T(8,128)(2,1)}), bf16[16,64,512]{2,1,0:T(8,128)(2,1)S(1)}, u32[]{:S(2)}, u32[]{:S(2)}) async-start(bf16[16,64,512]{2,1,0:T(8,128)(2,1)} %keys.1), calls=%async_computation | async-start | bytes 2097152 | tf_op jit(solution)/shard_map/all_to_all | solution.py:286
  12.9 2.9 %copy-start.3 = (bf16[4096]{0:T(1024)(128)(2,1)S(1)}, bf16[4096]{0:T(1024)(128)(2,1)}, u32[]{:S(2)}) copy-start(bf16[4096]{0:T(1024)(128)(2,1)} %param.17) | copy-start | bytes 24580
  15.8 3.0 %copy-start.5 = (s32[8]{0:T(128)S(1)}, s32[8]{0:T(128)}, u32[]{:S(2)}) copy-start(s32[8]{0:T(128)} %target_length.1) | copy-start | bytes 100
  15.8 1.6 %copy-start.1 = (bf16[64,16,1024]{2,1,0:T(8,128)(2,1)S(1)}, bf16[64,16,1024]{2,1,0:T(8,128)(2,1)}, u32[]{:S(2)}) copy-start(bf16[64,16,1024]{2,1,0:T(8,128)(2,1)} %param.12) | copy-start | bytes 6291460
  17.4 1.3 %copy-start.8 = (s32[8,8]{1,0:T(8,128)S(1)}, s32[8,8]{1,0:T(8,128)}, u32[]{:S(2)}) copy-start(s32[8,8]{1,0:T(8,128)} %param.14) | copy-start | bytes 772
  17.4 1.3 %copy-start.2 = (bf16[8,32,1024]{2,1,0:T(8,128)(2,1)S(1)}, bf16[8,32,1024]{2,1,0:T(8,128)(2,1)}, u32[]{:S(2)}) copy-start(bf16[8,32,1024]{2,1,0:T(8,128)(2,1)} %states_ref.1) | copy-start | bytes 1572868
  17.4 1.3 %copy-start.4 = (bf16[4096]{0:T(1024)(128)(2,1)S(1)}, bf16[4096]{0:T(1024)(128)(2,1)}, u32[]{:S(2)}) copy-start(bf16[4096]{0:T(1024)(128)(2,1)} %param.16) | copy-start | bytes 24580
  18.8 3.4 %copy-start = (bf16[8,8,16,4096]{3,2,1,0:T(8,128)(2,1)S(1)}, bf16[8,8,16,4096]{3,2,1,0:T(8,128)(2,1)}, u32[]{:S(2)}) copy-start(bf16[8,8,16,4096]{3,2,1,0:T(8,128)(2,1)} %param.9) | copy-start | bytes 25165828

commit v8 on v7

--- a/solution.py
+++ b/solution.py
@@ -22,12 +22,11 @@
 f32 = jnp.float32
 
 
-def turned(i, count, flip):
-    return ((i + count // 2) % count) ^ flip
-
-
-def place_of(device, count, flip):
-    return ((device ^ flip) + count // 2) % count
+def turned(i, count):
+    quarter = count // 4
+    which = i // quarter
+    which = 2 * (which == 0) + 1 * (which == 1) + 3 * (which == 2)
+    return (which * quarter + i % quarter) ^ BACK_FLIP
 
 
 def mirrored(i, count):
@@ -220,7 +219,7 @@
     if rows < PACKED:
         out_ref[...] = jnp.zeros_like(out_ref)
     for i in range(peers):
-        p = turned(i, peers, BACK_FLIP)
+        p = turned(i, peers)
         for r in range(rows):
             out_ref[i, pl.ds(r, PACKED, stride=PACKED), :] = pooled_ref[
                 pl.ds(place_ref[1, p * rows + r], PACKED, stride=slots), :
@@ -232,7 +231,7 @@
     total = total[:, :SUBLANES] + total[:, SUBLANES:] + first_ref[...]
     total = jnp.sum(total, axis=2, keepdims=True)
     shape = (total.shape[0], SUBLANES, LANES)
-    at = turned(iota(shape, 0), shape[0], BACK_FLIP) * rows + iota(shape, 1) % PACKED
+    at = turned(iota(shape, 0), shape[0]) * rows + iota(shape, 1) % PACKED
     total = jnp.where((iota(shape, 2) == at) & (iota(shape, 1) % PACKED < rows), total, 0.0)
     total = jnp.sum(jnp.sum(total, axis=0), axis=0, keepdims=True)
     out_ref[...] = total[:, : out_ref.shape[1]]
@@ -281,12 +280,11 @@
     )(pltpu.with_memory_space_constraint(candidate_states.reshape(peers, body, 2 * width), pltpu.HBM))
     assert peers % 16 == 0
     out_order = [mirrored(i, peers) ^ OUT_FLIP for i in range(peers)]
-    back_order = [turned(i, peers, BACK_FLIP) for i in range(peers)]
+    back_order = [turned(i, peers) for i in range(peers)]
     exchange = functools.partial(lax.all_to_all, axis_name="dp", split_axis=0, concat_axis=0, tiled=True)
     arrived = exchange(sent, axis_index_groups=[out_order])
 
     step = peers // 4
-    half = 2
     factor, first = pl.pallas_call(
         functools.partial(value_kernel, rows, keys),
         out_shape=(
@@ -299,8 +297,8 @@
             pl.BlockSpec((heads, HEAD_SIZE), lambda i: (0, 0)),
         ],
         out_specs=(
-            pl.BlockSpec((step, keys, LANES), lambda i: ((i + half) % (2 * half), 0, 0)),
-            pl.BlockSpec((step, SUBLANES, LANES), lambda i: ((i + half) % (2 * half), 0, 0)),
+            pl.BlockSpec((step, keys, LANES), lambda i: (3 * (i == 0) + 1 * (i == 1) + 2 * (i == 3), 0, 0)),
+            pl.BlockSpec((step, SUBLANES, LANES), lambda i: (3 * (i == 0) + 1 * (i == 1) + 2 * (i == 3), 0, 0)),
         ),
         scratch_shapes=[pltpu.VMEM((step * body, LANES), f32)],
         compiler_params=pltpu.CompilerParams(vmem_limit_bytes=16 * 2**20),

time: 45.5 us -> 45.5 us (level)
  no operation moved by 1% of the time
where the time goes in v8:
time: 45.5 us; the launch traced here: 44.9 us
  Pallas kernels  12.5 us (27%)
  local copies, waits for them, and re-layouts  10.4 us (23%)
  blocking collectives  8.29 us (18%)
  starting transfers between devices  7.98 us (18%)
  waiting for transfers between devices  5.39 us (12%)
    all_to_all x1, blocking collectives, on_device(): returned = exchange(outgoing, axis_index_groups=[back_order])  8.29 us
    all_to_all x1, starting transfers between devices, on_device(): arrived = exchange(sent, axis_index_groups=[out_order])  7.98 us
    pallas_call x1, Pallas kernels, on_device(): pl.pallas_call(direct_kernel, out_shape=(jax.ShapeDtypeStruct((targets, s...  6.02 us
    unnamed x19, local copies, waits for them, and re-layouts  5.48 us
    all_to_all x1, waiting for transfers between devices, on_device(): arrived = exchange(sent, axis_index_groups=[out_order])  5.39 us
    reshape x1, local copies, waits for them, and re-layouts, on_device(): queries.transpose(0, 2, 4, 1, 3)  2.87 us
    pallas_call x1, Pallas kernels, on_device(): pl.pallas_call(keys_kernel, out_shape=jax.ShapeDtypeStruct((peers, body,...  2.39 us
    pallas_call x1, Pallas kernels, on_device(): pl.pallas_call(functools.partial(channel_kernel, rows), out_shape=jax.Sha...  2.37 us
  transfers between devices with their start and end apart: 1, of which 1 were waited for; matrix products, arithmetic and copies ran while one was open for 13% of the time, Pallas kernels for 16%

profile of v8, /device:TPU:0, one launch (start us, length us, event | category | flops | bytes accessed | tf_op | source)
XLA Modules:
  0.0 44.9 jit_solution(11053726267094126277)
XLA Ops:
  0.0 2.4 %keys.1 = bf16[16,64,512]{2,1,0:T(8,128)(2,1)} custom-call(bf16[16,64,1024]{2,1,0:T(8,128)(2,1)} %bitcast.17), custom_call_target="tpu_custom_call" | custom-call | tf_op jit(solution)/shard_map/keys/pallas_call | solution.py:269
  2.4 8.0 %all-to-all-start = ((bf16[16,64,512]{2,1,0:T(8,128)(2,1)}), bf16[16,64,512]{2,1,0:T(8,128)(2,1)S(1)}, u32[]{:S(2)}, u32[]{:S(2)}) async-start(bf16[16,64,512]{2,1,0:T(8,128)(2,1)} %keys.1), calls=%async_computation | async-start | bytes 2097152 | tf_op jit(solution)/shard_map/all_to_all | solution.py:285
  10.4 0.0 copy-done.7
  10.4 0.1 eq.20
  10.5 0.1 reshape.306
  10.5 0.5 %copy.16 = bf16[32,8,32,128]{3,2,1,0:T(8,128)(2,1)S(1)} copy(bf16[32,8,32,128]{3,1,2,0:T(8,128)(2,1)S(1)} %bitcast.24) | data formatting | bytes 4194304
  11.0 1.9 %copy.18 = bf16[8,4,128,32,8]{2,4,3,1,0:T(8,128)(2,1)} copy(bf16[8,4,128,32,8]{2,4,1,3,0:T(8,128)(2,1)S(1)} %bitcast.23) | data formatting | bytes 4194304 | tf_op jit(solution)/shard_map/transpose | solution.py:360
  12.9 2.9 %copy.15.queries_ref = bf16[8,4,128,256]{3,2,1,0:T(8,128)(2,1)S(1)} copy(bf16[8,4,128,256]{2,3,1,0:T(8,128)(2,1)} %bitcast.22) | data formatting | bytes 4194304 | tf_op jit(solution)/shard_map/reshape | solution.py:360
  15.8 0.0 copy-start.5
  15.8 0.0 copy-start.1
  15.8 1.6 %copy-done.1 = bf16[64,16,1024]{2,1,0:T(8,128)(2,1)S(1)} copy-done((bf16[64,16,1024]{2,1,0:T(8,128)(2,1)S(1)}, bf16[64,16,1024]{2,1,0:T(8,128)(2,1)}, u32[]{:S(2)}) %copy-start.1) | copy-done | bytes 2097176
  17.4 1.1 %value.1 = (f32[16,16,128]{2,1,0:T(8,128)S(1)}, f32[16,8,128]{2,1,0:T(8,128)S(1)}) custom-call(bf16[16,64,1024]{2,1,0:T(8,128)(2,1)S(1)} %bitcast.18, bf16[32,128]{1,0:T(8,128)(2,1)S(1)} %bitcast.20), custom_call_target="tpu_custom_call" | custom-call | flops 134217728 | bytes 1048576 | tf_op jit(solution)/shard_map/value/pallas_call | solution.py:288
  18.5 0.1 select_reduce_fusion
  18.7 0.0 copy-done.8
  18.7 0.1 broadcast_in_dim.36.length_ref
  18.7 0.0 copy-done.2
  18.8 0.0 copy-start
  18.8 3.4 %copy-done = bf16[8,8,16,4096]{3,2,1,0:T(8,128)(2,1)S(1)} copy-done((bf16[8,8,16,4096]{3,2,1,0:T(8,128)(2,1)S(1)}, bf16[8,8,16,4096]{3,2,1,0:T(8,128)(2,1)}, u32[]{:S(2)}) %copy-start) | copy-done | bytes 8388632
  22.1 6.0 %direct.1 = (f32[8,8,128]{2,1,0:T(8,128)S(1)}, s32[2,64]{1,0:T(2,128)S(4)}) custom-call(s32[8]{0:T(128)S(1)} %copy-done.5, s32[2,64]{1,0:T(2,128)S(1)} %pad_add_fusion.at_ref, bf16[8,128,4096]{2,1,0:T(8,128)(2,1)S(1)} %bitcast.16, bf16[8,32,1024]{2,1,0:T(8,128)(2,1)S(1)} %copy-done.2, bf16[32,128]{1,0:T(8,128)(2,1)S(1)} %bitcast.21, ...), custom_call_target="tpu_custom_call" | custom-call | flops 536870912 | bytes 8388608 | tf_op jit(solution)/shard_map/direct/pallas_call | solution.py:323
  28.2 0.1 compare_select_fusion.weight_ref
  28.3 5.4 %all-to-all-done = bf16[16,64,512]{2,1,0:T(8,128)(2,1)S(1)} async-done(((bf16[16,64,512]{2,1,0:T(8,128)(2,1)}), bf16[16,64,512]{2,1,0:T(8,128)(2,1)S(1)}, u32[]{:S(2)}, u32[]{:S(2)}) %all-to-all-start) | async-done | bytes 1048608 | tf_op jit(solution)/shard_map/all_to_all | solution.py:285
  33.6 2.4 %channel.1 = f32[16,16,128]{2,1,0:T(8,128)S(1)} custom-call(s32[2,64]{1,0:T(2,128)S(4)} %get-tuple-element.12.place_ref, bf16[1024,512]{1,0:T(8,128)(2,1)S(1)} %bitcast.19, bf16[8,4,128,256]{3,2,1,0:T(8,128)(2,1)S(1)} %copy.15.queries_ref, f32[8,8,128]{2,1,0:T(8,128)S(1)} %get-tuple-element.16.direct_ref, s32[8,8,128]{2,1,0:T(8,128)S(1)} %broadcast_in_dim.36.length_ref, ...), custom_call_target="tpu_custom_call" | custom-call | tf_op jit(solution)/shard_map/channel/pallas_call | solution.py:367
  36.0 8.3 %all_to_all.10.returned_ref = f32[16,16,128]{2,1,0:T(8,128)S(1)} all-to-all(f32[16,16,128]{2,1,0:T(8,128)S(1)} %channel.1), channel_id=1, replica_groups={{11,10,9,8,7,6,5,4,15,14,13,12,3,2,1,0},{27,26,25,24,23,22,21,20,31,30,..., dimensions={0} | all-to-all | bytes 262144 | tf_op jit(solution)/shard_map/all_to_all | solution.py:386
  44.3 0.6 %finish.1 = f32[1,64]{1,0:T(1,128)} custom-call(f32[16,16,128]{2,1,0:T(8,128)S(1)} %all_to_all.10.returned_ref, f32[16,16,128]{2,1,0:T(8,128)S(1)} %get-tuple-element.17.factor_ref, f32[16,8,128]{2,1,0:T(8,128)S(1)} %get-tuple-element.18.first_ref), custom_call_target="tpu_custom_call" | custom-call | tf_op jit(solution)/shard_map/finish/pallas_call | solution.py:387
  (15 shorter events, 0.1 us)
Async XLA Ops:
  0.0 10.4 %copy-start.7 = (s32[8,8]{1,0:T(8,128)S(1)}, s32[8,8]{1,0:T(8,128)}, u32[]{:S(2)}) copy-start(s32[8,8]{1,0:T(8,128)} %param.15) | copy-start | bytes 772
  0.0 10.5 %copy-start.6 = (bf16[8,32,4096]{2,1,0:T(8,128)(2,1)S(1)}, bf16[8,32,4096]{2,1,0:T(8,128)(2,1)}, u32[]{:S(2)}) copy-start(bf16[8,32,4096]{2,1,0:T(8,128)(2,1)} %param.11) | copy-start | bytes 6291460
  2.4 31.2 %all-to-all-start = ((bf16[16,64,512]{2,1,0:T(8,128)(2,1)}), bf16[16,64,512]{2,1,0:T(8,128)(2,1)S(1)}, u32[]{:S(2)}, u32[]{:S(2)}) async-start(bf16[16,64,512]{2,1,0:T(8,128)(2,1)} %keys.1), calls=%async_computation | async-start | bytes 2097152 | tf_op jit(solution)/shard_map/all_to_all | solution.py:285
  12.9 2.9 %copy-start.3 = (bf16[4096]{0:T(1024)(128)(2,1)S(1)}, bf16[4096]{0:T(1024)(128)(2,1)}, u32[]{:S(2)}) copy-start(bf16[4096]{0:T(1024)(128)(2,1)} %param.17) | copy-start | bytes 24580
  15.8 3.0 %copy-start.5 = (s32[8]{0:T(128)S(1)}, s32[8]{0:T(128)}, u32[]{:S(2)}) copy-start(s32[8]{0:T(128)} %target_length.1) | copy-start | bytes 100
  15.8 1.6 %copy-start.1 = (bf16[64,16,1024]{2,1,0:T(8,128)(2,1)S(1)}, bf16[64,16,1024]{2,1,0:T(8,128)(2,1)}, u32[]{:S(2)}) copy-start(bf16[64,16,1024]{2,1,0:T(8,128)(2,1)} %param.12) | copy-start | bytes 6291460
  17.4 1.3 %copy-start.8 = (s32[8,8]{1,0:T(8,128)S(1)}, s32[8,8]{1,0:T(8,128)}, u32[]{:S(2)}) copy-start(s32[8,8]{1,0:T(8,128)} %param.14) | copy-start | bytes 772
  17.4 1.3 %copy-start.2 = (bf16[8,32,1024]{2,1,0:T(8,128)(2,1)S(1)}, bf16[8,32,1024]{2,1,0:T(8,128)(2,1)}, u32[]{:S(2)}) copy-start(bf16[8,32,1024]{2,1,0:T(8,128)(2,1)} %states_ref.1) | copy-start | bytes 1572868
  17.4 1.3 %copy-start.4 = (bf16[4096]{0:T(1024)(128)(2,1)S(1)}, bf16[4096]{0:T(1024)(128)(2,1)}, u32[]{:S(2)}) copy-start(bf16[4096]{0:T(1024)(128)(2,1)} %param.16) | copy-start | bytes 24580
  18.8 3.4 %copy-start = (bf16[8,8,16,4096]{3,2,1,0:T(8,128)(2,1)S(1)}, bf16[8,8,16,4096]{3,2,1,0:T(8,128)(2,1)}, u32[]{:S(2)}) copy-start(bf16[8,8,16,4096]{3,2,1,0:T(8,128)(2,1)} %param.9) | copy-start | bytes 25165828

commit v9 on v7

--- a/solution.py
+++ b/solution.py
@@ -15,7 +15,7 @@
 MASKED = -1e30
 PACKED = 4
 KEY_PARTS = 4
-OUT_FLIP = 3
+OUT_FLIP = 0
 BACK_FLIP = 3
 
 bf16 = jnp.bfloat16

time: 45.5 us -> 46.1 us (1.013)
  blocking collectives: 8.29 us -> 9.91 us
  waiting for transfers between devices: 5.39 us -> 4.65 us
    all_to_all x1, blocking collectives: 8.29 us -> 9.91 us  [on_device(): returned = exchange(outgoing, axis_index_groups=[back_order])]
    all_to_all x1, waiting for transfers between devices: 5.39 us -> 4.65 us  [on_device(): arrived = exchange(sent, axis_index_groups=[out_order])]
where the time goes in v9:
time: 46.1 us; the launch traced here: 45.5 us
  Pallas kernels  12.3 us (27%)
  local copies, waits for them, and re-layouts  10.4 us (23%)
  blocking collectives  9.91 us (21%)
  starting transfers between devices  7.87 us (17%)
  waiting for transfers between devices  4.65 us (10%)
    all_to_all x1, blocking collectives, on_device(): returned = exchange(outgoing, axis_index_groups=[back_order])  9.91 us
    all_to_all x1, starting transfers between devices, on_device(): arrived = exchange(sent, axis_index_groups=[out_order])  7.87 us
    pallas_call x1, Pallas kernels, on_device(): pl.pallas_call(direct_kernel, out_shape=(jax.ShapeDtypeStruct((targets, s...  6.02 us
    unnamed x19, local copies, waits for them, and re-layouts  5.48 us
    all_to_all x1, waiting for transfers between devices, on_device(): arrived = exchange(sent, axis_index_groups=[out_order])  4.65 us
    reshape x1, local copies, waits for them, and re-layouts, on_device(): queries.transpose(0, 2, 4, 1, 3)  2.87 us
    pallas_call x1, Pallas kernels, on_device(): pl.pallas_call(functools.partial(channel_kernel, rows), out_shape=jax.Sha...  2.37 us
    pallas_call x1, Pallas kernels, on_device(): pl.pallas_call(keys_kernel, out_shape=jax.ShapeDtypeStruct((peers, body,...  2.19 us
  transfers between devices with their start and end apart: 1, of which 1 were waited for; matrix products, arithmetic and copies ran while one was open for 13% of the time, Pallas kernels for 16%

profile of v9, /device:TPU:0, one launch (start us, length us, event | category | flops | bytes accessed | tf_op | source)
XLA Modules:
  0.0 45.5 jit_solution(7376468654884864875)
XLA Ops:
  0.0 2.2 %keys.1 = bf16[16,64,512]{2,1,0:T(8,128)(2,1)} custom-call(bf16[16,64,1024]{2,1,0:T(8,128)(2,1)} %bitcast.17), custom_call_target="tpu_custom_call" | custom-call | tf_op jit(solution)/shard_map/keys/pallas_call | solution.py:270
  2.2 7.9 %all-to-all-start = ((bf16[16,64,512]{2,1,0:T(8,128)(2,1)}), bf16[16,64,512]{2,1,0:T(8,128)(2,1)S(1)}, u32[]{:S(2)}, u32[]{:S(2)}) async-start(bf16[16,64,512]{2,1,0:T(8,128)(2,1)} %keys.1), calls=%async_computation | async-start | bytes 2097152 | tf_op jit(solution)/shard_map/all_to_all | solution.py:286
  10.1 0.0 copy-done.7
  10.1 0.1 eq.20
  10.2 0.1 reshape.303
  10.2 0.5 %copy.16 = bf16[32,8,32,128]{3,2,1,0:T(8,128)(2,1)S(1)} copy(bf16[32,8,32,128]{3,1,2,0:T(8,128)(2,1)S(1)} %bitcast.24) | data formatting | bytes 4194304
  10.7 1.9 %copy.18 = bf16[8,4,128,32,8]{2,4,3,1,0:T(8,128)(2,1)} copy(bf16[8,4,128,32,8]{2,4,1,3,0:T(8,128)(2,1)S(1)} %bitcast.23) | data formatting | bytes 4194304 | tf_op jit(solution)/shard_map/transpose | solution.py:362
  12.6 2.9 %copy.15.queries_ref = bf16[8,4,128,256]{3,2,1,0:T(8,128)(2,1)S(1)} copy(bf16[8,4,128,256]{2,3,1,0:T(8,128)(2,1)} %bitcast.22) | data formatting | bytes 4194304 | tf_op jit(solution)/shard_map/reshape | solution.py:362
  15.5 0.0 copy-start.5
  15.5 0.0 copy-start.1
  15.5 1.6 %copy-done.1 = bf16[64,16,1024]{2,1,0:T(8,128)(2,1)S(1)} copy-done((bf16[64,16,1024]{2,1,0:T(8,128)(2,1)S(1)}, bf16[64,16,1024]{2,1,0:T(8,128)(2,1)}, u32[]{:S(2)}) %copy-start.1) | copy-done | bytes 2097176
  17.1 1.1 %value.1 = (f32[16,16,128]{2,1,0:T(8,128)S(1)}, f32[16,8,128]{2,1,0:T(8,128)S(1)}) custom-call(bf16[16,64,1024]{2,1,0:T(8,128)(2,1)S(1)} %bitcast.18, bf16[32,128]{1,0:T(8,128)(2,1)S(1)} %bitcast.20), custom_call_target="tpu_custom_call" | custom-call | flops 134217728 | bytes 1048576 | tf_op jit(solution)/shard_map/value/pallas_call | solution.py:290
  18.2 0.1 select_reduce_fusion
  18.4 0.0 copy-done.8
  18.4 0.1 broadcast_in_dim.36.length_ref
  18.4 0.0 copy-done.2
  18.5 0.0 copy-start
  18.5 3.4 %copy-done = bf16[8,8,16,4096]{3,2,1,0:T(8,128)(2,1)S(1)} copy-done((bf16[8,8,16,4096]{3,2,1,0:T(8,128)(2,1)S(1)}, bf16[8,8,16,4096]{3,2,1,0:T(8,128)(2,1)}, u32[]{:S(2)}) %copy-start) | copy-done | bytes 8388632
  21.8 6.0 %direct.1 = (f32[8,8,128]{2,1,0:T(8,128)S(1)}, s32[2,64]{1,0:T(2,128)S(4)}) custom-call(s32[8]{0:T(128)S(1)} %copy-done.5, s32[2,64]{1,0:T(2,128)S(1)} %pad_add_fusion.at_ref, bf16[8,128,4096]{2,1,0:T(8,128)(2,1)S(1)} %bitcast.16, bf16[8,32,1024]{2,1,0:T(8,128)(2,1)S(1)} %copy-done.2, bf16[32,128]{1,0:T(8,128)(2,1)S(1)} %bitcast.21, ...), custom_call_target="tpu_custom_call" | custom-call | flops 536870912 | bytes 8388608 | tf_op jit(solution)/shard_map/direct/pallas_call | solution.py:325
  27.9 0.1 compare_select_fusion.weight_ref
  27.9 4.7 %all-to-all-done = bf16[16,64,512]{2,1,0:T(8,128)(2,1)S(1)} async-done(((bf16[16,64,512]{2,1,0:T(8,128)(2,1)}), bf16[16,64,512]{2,1,0:T(8,128)(2,1)S(1)}, u32[]{:S(2)}, u32[]{:S(2)}) %all-to-all-start) | async-done | bytes 1048608 | tf_op jit(solution)/shard_map/all_to_all | solution.py:286
  32.6 2.4 %channel.1 = f32[16,16,128]{2,1,0:T(8,128)S(1)} custom-call(s32[2,64]{1,0:T(2,128)S(4)} %get-tuple-element.12.place_ref, bf16[1024,512]{1,0:T(8,128)(2,1)S(1)} %bitcast.19, bf16[8,4,128,256]{3,2,1,0:T(8,128)(2,1)S(1)} %copy.15.queries_ref, f32[8,8,128]{2,1,0:T(8,128)S(1)} %get-tuple-element.16.direct_ref, s32[8,8,128]{2,1,0:T(8,128)S(1)} %broadcast_in_dim.36.length_ref, ...), custom_call_target="tpu_custom_call" | custom-call | tf_op jit(solution)/shard_map/channel/pallas_call | solution.py:369
  35.0 9.9 %all_to_all.10.returned_ref = f32[16,16,128]{2,1,0:T(8,128)S(1)} all-to-all(f32[16,16,128]{2,1,0:T(8,128)S(1)} %channel.1), channel_id=1, replica_groups={{11,10,9,8,15,14,13,12,3,2,1,0,7,6,5,4},{27,26,25,24,31,30,29,28,19,18,..., dimensions={0} | all-to-all | bytes 262144 | tf_op jit(solution)/shard_map/all_to_all | solution.py:388
  44.9 0.6 %finish.1 = f32[1,64]{1,0:T(1,128)} custom-call(f32[16,16,128]{2,1,0:T(8,128)S(1)} %all_to_all.10.returned_ref, f32[16,16,128]{2,1,0:T(8,128)S(1)} %get-tuple-element.17.factor_ref, f32[16,8,128]{2,1,0:T(8,128)S(1)} %get-tuple-element.18.first_ref), custom_call_target="tpu_custom_call" | custom-call | tf_op jit(solution)/shard_map/finish/pallas_call | solution.py:389
  (15 shorter events, 0.1 us)
Async XLA Ops:
  0.0 10.1 %copy-start.7 = (s32[8,8]{1,0:T(8,128)S(1)}, s32[8,8]{1,0:T(8,128)}, u32[]{:S(2)}) copy-start(s32[8,8]{1,0:T(8,128)} %param.15) | copy-start | bytes 772
  0.0 10.2 %copy-start.6 = (bf16[8,32,4096]{2,1,0:T(8,128)(2,1)S(1)}, bf16[8,32,4096]{2,1,0:T(8,128)(2,1)}, u32[]{:S(2)}) copy-start(bf16[8,32,4096]{2,1,0:T(8,128)(2,1)} %param.11) | copy-start | bytes 6291460
  2.2 30.4 %all-to-all-start = ((bf16[16,64,512]{2,1,0:T(8,128)(2,1)}), bf16[16,64,512]{2,1,0:T(8,128)(2,1)S(1)}, u32[]{:S(2)}, u32[]{:S(2)}) async-start(bf16[16,64,512]{2,1,0:T(8,128)(2,1)} %keys.1), calls=%async_computation | async-start | bytes 2097152 | tf_op jit(solution)/shard_map/all_to_all | solution.py:286
  12.6 2.9 %copy-start.3 = (bf16[4096]{0:T(1024)(128)(2,1)S(1)}, bf16[4096]{0:T(1024)(128)(2,1)}, u32[]{:S(2)}) copy-start(bf16[4096]{0:T(1024)(128)(2,1)} %param.17) | copy-start | bytes 24580
  15.5 3.0 %copy-start.5 = (s32[8]{0:T(128)S(1)}, s32[8]{0:T(128)}, u32[]{:S(2)}) copy-start(s32[8]{0:T(128)} %target_length.1) | copy-start | bytes 100
  15.5 1.6 %copy-start.1 = (bf16[64,16,1024]{2,1,0:T(8,128)(2,1)S(1)}, bf16[64,16,1024]{2,1,0:T(8,128)(2,1)}, u32[]{:S(2)}) copy-start(bf16[64,16,1024]{2,1,0:T(8,128)(2,1)} %param.12) | copy-start | bytes 6291460
  17.1 1.3 %copy-start.8 = (s32[8,8]{1,0:T(8,128)S(1)}, s32[8,8]{1,0:T(8,128)}, u32[]{:S(2)}) copy-start(s32[8,8]{1,0:T(8,128)} %param.14) | copy-start | bytes 772
  17.1 1.3 %copy-start.2 = (bf16[8,32,1024]{2,1,0:T(8,128)(2,1)S(1)}, bf16[8,32,1024]{2,1,0:T(8,128)(2,1)}, u32[]{:S(2)}) copy-start(bf16[8,32,1024]{2,1,0:T(8,128)(2,1)} %states_ref.1) | copy-start | bytes 1572868
  17.1 1.3 %copy-start.4 = (bf16[4096]{0:T(1024)(128)(2,1)S(1)}, bf16[4096]{0:T(1024)(128)(2,1)}, u32[]{:S(2)}) copy-start(bf16[4096]{0:T(1024)(128)(2,1)} %param.16) | copy-start | bytes 24580
  18.5 3.4 %copy-start = (bf16[8,8,16,4096]{3,2,1,0:T(8,128)(2,1)S(1)}, bf16[8,8,16,4096]{3,2,1,0:T(8,128)(2,1)}, u32[]{:S(2)}) copy-start(bf16[8,8,16,4096]{3,2,1,0:T(8,128)(2,1)} %param.9) | copy-start | bytes 25165828
